TPU v7x, 128 devices: a whole 4x4x4 slice. The times are simulated.
128 devices in a mesh: role: 4 (over z_hi, core), shard: 32 (over y, x, z_lo).
Axes of the slice: x: 4, y: 4, z: 4 (z_hi: 2, z_lo: 2; z = z_hi * 2 + z_lo), core: 2. Of those that a mesh axis runs over, the one named last changes fastest.
Arguments:
- action_ids: int32 [128, 8], P(('role', 'shard')), may hold values from 0 to 255
- traj_lengths: int32 [128], P(('role', 'shard')), may hold values from 1 to 8
- action_table: bfloat16 [256, 4096], P(None, 'shard'), may hold values from -6 to 6
- prefix_keys: bfloat16 [128, 128, 2048], P(('role', 'shard')), may hold values from -6 to 6
- prefix_values: bfloat16 [128, 128, 2048], P(('role', 'shard')), may hold values from -6 to 6
- qkv_weight: bfloat16 [4096, 6144], P('shard'), may hold values from -0.09375 to 0.09375
- out_weight: bfloat16 [2048, 4096], P(None, 'shard'), may hold values from -0.125 to 0.125
- first_qkv: float32 [4096, 6144], P('shard', 'role'), may hold values from -6 to 6
- second_qkv: float32 [4096, 6144], P('shard', 'role'), may hold values from 1 to 100
- first_out: float32 [2048, 4096], P('role', 'shard'), may hold values from -6 to 6
- second_out: float32 [2048, 4096], P('role', 'shard'), may hold values from 1 to 100
- out_cotangent: bfloat16 [1024, 4096], P('role', 'shard'), may hold values from -6 to 6
Outputs:
- decoded: bfloat16 [1024, 4096], P('role', 'shard')
- new_qkv: bfloat16 [4096, 6144], P('shard')
- new_out: bfloat16 [2048, 4096], P(None, 'shard')
- moment_qkv: float32 [4096, 6144], P('shard', 'role')
- square_qkv: float32 [4096, 6144], P('shard', 'role')
- moment_out: float32 [2048, 4096], P('role', 'shard')
- square_out: float32 [2048, 4096], P('role', 'shard')
All inputs are finite; a program needn't handle non-finite values.
Results may differ from a plain program's by a relative error of at most 0.0071.
Values may be sent and summed in bfloat16 or wider, within the bound.
A program may use at most 64 MiB of HBM per device.

v0:
```python
import jax
import jax.numpy as jnp
from jax import lax
from jax.sharding import Mesh
from jax.sharding import PartitionSpec as P

HD = 128
SHARD = ("shard_0", "shard_1", "shard_2")
ROLE_SHARD = ("role", "shard_0", "shard_1", "shard_2")


learn_rate = 0.001
first_decay = 0.9
second_decay = 0.95
adam_eps = 1e-08
weight_decay = 0.1
first_fix = 1.0 - 0.9**10
second_fix = 1.0 - 0.95**10


def side_by_side(arrays, axis, dim, along):
    columns = [a.reshape(*a.shape[:along], -1) for a in arrays]
    both = jnp.concatenate(columns, axis=along)
    filled, at, finished = (lax.all_gather(both, axis, axis=dim, tiled=True), 0, [])
    for a, column in zip(arrays, columns):
        slab = filled[..., at : at + column.shape[along]]
        finished.append(slab.reshape(*slab.shape[:along], *a.shape[along:]))
        at += column.shape[along]
    return tuple(finished)


def from_everyone(array, axis):
    copies = jnp.broadcast_to(array, (lax.axis_size(axis), *array.shape))
    return lax.all_to_all(copies, axis, split_axis=0, concat_axis=0, tiled=True)


def laid_out(tiles, dim):
    dims = list(tiles.shape[1:])
    dims[dim] *= tiles.shape[0]
    return jnp.moveaxis(tiles, 0, dim).reshape(dims)


def gather_directly(array, axis, dim):
    tiles = from_everyone(array, axis)
    return laid_out(tiles, dim)


def in_blocks(array, dim, size):
    before, after = (array.shape[:dim], array.shape[dim + 1 :])
    return jnp.moveaxis(array.reshape(*before, size, -1, *after), dim, 0)


def sent_and_summed(array, axis, dim):
    tiles = in_blocks(array, dim, lax.axis_size(axis))
    arrived = lax.all_to_all(tiles, axis, split_axis=0, concat_axis=0, tiled=True)
    return arrived.sum(axis=0)


def gather_in_order(array, axes, order):
    tiles = array
    for k in order:
        tiles = lax.all_gather(tiles, axes[k])
    done = order[::-1]
    back = [done.index(k) for k in range(len(axes))]
    tiles = tiles.transpose(*back, *range(len(axes), tiles.ndim))
    return tiles.reshape(-1, *array.shape)


def gather_axes(array, axes, order, dim):
    return laid_out(gather_in_order(array, axes, order), dim)


def sum_packed(arrays, axis, dims):
    size = lax.axis_size(axis)
    tiles = [in_blocks(a, dim, size) for a, dim in zip(arrays, dims)]
    lines = jnp.concatenate([b.reshape(size, -1) for b in tiles], axis=1)
    rows = max(16, -(-lines.shape[1] // 1024) * 8)
    lines = jnp.pad(lines, ((0, 0), (0, rows * 128 - lines.shape[1]))).reshape(-1, 128)
    ravelled, at, finished = (lax.psum_scatter(lines, axis, tiled=True).reshape(-1), 0, [])
    for b in tiles:
        part = b[0]
        finished.append(ravelled[at : at + part.size].reshape(part.shape))
        at += part.size
    return tuple(finished)


def unpack(qkv_rows, keys_pre, vals_pre):
    span_width = keys_pre.shape[-1]
    head_count = span_width // HD
    positions = qkv_rows.shape[0]
    total_keys = keys_pre.shape[0] + positions
    queries = qkv_rows[:, :span_width].astype(jnp.float32).reshape(positions, head_count, HD)
    all_keys = (
        jnp.concatenate([keys_pre, qkv_rows[:, span_width : 2 * span_width]], 0)
        .astype(jnp.float32)
        .reshape(total_keys, head_count, HD)
    )
    all_values = (
        jnp.concatenate([vals_pre, qkv_rows[:, 2 * span_width :]], 0)
        .astype(jnp.float32)
        .reshape(total_keys, head_count, HD)
    )
    return (queries, all_keys, all_values)


def attend(qkv_rows, keys_pre, vals_pre, length):
    queries, all_keys, all_values = unpack(qkv_rows, keys_pre, vals_pre)
    prefix_len = keys_pre.shape[0]
    positions = qkv_rows.shape[0]
    attn_scale = HD ** (-0.5)
    scores = jnp.einsum("thd,lhd->htl", queries, all_keys) * attn_scale
    position = jnp.arange(positions, dtype=jnp.int32)[:, None]
    offset = jnp.arange(prefix_len + positions, dtype=jnp.int32)[None, :] - prefix_len
    allowed = (offset < 0) | (offset <= position) & (offset < length)
    scores = jnp.where(allowed[None], scores, -1e30)
    weights = jax.nn.softmax(scores, axis=-1)
    rounded = lax.optimization_barrier(weights.astype(jnp.bfloat16))
    head_mix = jnp.einsum("htl,lhd->thd", rounded.astype(jnp.float32), all_values)
    return (head_mix.reshape(positions, -1).astype(jnp.bfloat16), weights, rounded)


def attend_back(qkv_rows, keys_pre, vals_pre, weights, rounded, upstream):
    queries, all_keys, all_values = unpack(qkv_rows, keys_pre, vals_pre)
    prefix_len = keys_pre.shape[0]
    positions = qkv_rows.shape[0]
    attn_scale = HD ** (-0.5)
    grads_head = upstream.astype(jnp.float32).reshape(positions, -1, HD)
    grad_weights = jnp.einsum("thd,lhd->htl", grads_head, all_values)
    grad_scores = (
        weights
        * (grad_weights - jnp.sum(weights * grad_weights, axis=-1, keepdims=True))
        * attn_scale
    )
    grad_rounded = lax.optimization_barrier(grad_scores.astype(jnp.bfloat16)).astype(jnp.float32)
    grad_query = jnp.einsum("htl,lhd->thd", grad_rounded, all_keys).reshape(positions, -1)
    grad_key = jnp.einsum("htl,thd->lhd", grad_rounded[:, :, prefix_len:], queries).reshape(
        positions, -1
    )
    grad_value = jnp.einsum(
        "htl,thd->lhd", rounded.astype(jnp.float32)[:, :, prefix_len:], grads_head
    ).reshape(positions, -1)
    return jnp.concatenate([grad_query, grad_key, grad_value], 1).astype(jnp.bfloat16)


def adamw(params, gradient, first_moment, second_moment):
    moment_one = first_decay * first_moment + (1.0 - first_decay) * gradient
    moment_two = second_decay * second_moment + (1.0 - second_decay) * gradient * gradient
    stepped = moment_one / first_fix / (jnp.sqrt(moment_two / second_fix) + adam_eps)
    wide_params = params.astype(jnp.float32)
    updated = wide_params - learn_rate * (stepped + weight_decay * wide_params)
    return (updated, moment_one, moment_two)


def shards(
    action_ids,
    traj_lengths,
    action_table,
    prefix_keys,
    prefix_values,
    qkv_weight,
    out_weight,
    first_qkv,
    second_qkv,
    first_out,
    second_out,
    out_cotangent,
):
    own_episodes = action_ids.shape[0]
    horizon = action_ids.shape[1]
    own_rows = own_episodes * horizon
    contract_rows = (((0,), (0,)), ((), ()))
    group_ids, group_lengths = side_by_side((action_ids, traj_lengths), SHARD, 0, 1)
    onehot = (
        group_ids.reshape(-1)[:, None]
        == jnp.arange(action_table.shape[0], dtype=jnp.int32)[None, :]
    ).astype(jnp.bfloat16)
    inputs = jnp.dot(onehot, action_table, preferred_element_type=jnp.float32).astype(jnp.bfloat16)
    projected = lax.psum_scatter(
        jnp.dot(inputs, qkv_weight, preferred_element_type=jnp.float32),
        SHARD,
        scatter_dimension=0,
        tiled=True,
    ).astype(jnp.bfloat16)
    projected = projected.reshape(own_episodes, horizon, -1)
    head_mix, weights, rounded = jax.vmap(attend)(
        projected, prefix_keys, prefix_values, traj_lengths
    )
    head_rows = head_mix.reshape(own_rows, -1)
    valid = (jnp.arange(horizon, dtype=jnp.int32)[None, :] < group_lengths[:, None]).reshape(-1)
    masked = jnp.where(valid[:, None], out_cotangent, jnp.zeros_like(out_cotangent))
    gathered = gather_directly(head_rows, SHARD, 0)
    decoded = jnp.dot(gathered, out_weight, preferred_element_type=jnp.float32).astype(jnp.bfloat16)
    grad_out = lax.dot_general(gathered, masked, contract_rows, preferred_element_type=jnp.float32)
    grad_heads = sent_and_summed(
        lax.dot_general(
            masked, out_weight, (((1,), (1,)), ((), ())), preferred_element_type=jnp.float32
        ),
        SHARD,
        0,
    ).astype(jnp.bfloat16)
    grad_heads = grad_heads.reshape(own_episodes, horizon, -1)
    grad_proj = jax.vmap(attend_back)(
        projected, prefix_keys, prefix_values, weights, rounded, grad_heads
    ).reshape(own_rows, -1)
    grad_qkv = lax.dot_general(
        inputs,
        gather_axes(grad_proj, SHARD, (2, 0, 1), 0),
        contract_rows,
        preferred_element_type=jnp.float32,
    )
    learner = lax.axis_size("role") - 1
    role_index = lax.axis_index("role")
    qkv_part = first_qkv.shape[1]
    out_part = first_out.shape[0]
    is_learner = role_index == learner
    send_qkv = jnp.where(is_learner, grad_qkv, jnp.zeros_like(grad_qkv))
    send_out = jnp.where(is_learner, grad_out, jnp.zeros_like(grad_out))
    share_qkv, share_out = tuple(
        (
            part.astype(jnp.float32)
            for part in sum_packed(
                (send_qkv.astype(jnp.bfloat16), send_out.astype(jnp.bfloat16)), "role", (1, 0)
            )
        )
    )
    weight_qkv = lax.dynamic_slice_in_dim(qkv_weight, role_index * qkv_part, qkv_part, 1)
    weight_out = lax.dynamic_slice_in_dim(out_weight, role_index * out_part, out_part, 0)
    piece_qkv, moment_qkv, square_qkv = adamw(weight_qkv, share_qkv, first_qkv, second_qkv)
    piece_out, moment_out, square_out = adamw(weight_out, share_out, first_out, second_out)
    new_qkv, new_out = (
        gather_directly(piece_qkv.astype(jnp.bfloat16), "role", 1),
        gather_directly(piece_out.astype(jnp.bfloat16), "role", 0),
    )
    return (decoded, new_qkv, new_out, moment_qkv, square_qkv, moment_out, square_out)


def solution(mesh):
    split = Mesh(
        mesh.devices.reshape(mesh.shape["role"], 4, 4, 2), ("role", "shard_0", "shard_1", "shard_2")
    )
    return jax.shard_map(
        shards,
        mesh=split,
        in_specs=(
            P(ROLE_SHARD, None),
            P(ROLE_SHARD),
            P(None, SHARD),
            P(ROLE_SHARD, None, None),
            P(ROLE_SHARD, None, None),
            P(SHARD, None),
            P(None, SHARD),
            P(SHARD, "role"),
            P(SHARD, "role"),
            P("role", SHARD),
            P("role", SHARD),
            P("role", SHARD),
        ),
        out_specs=(
            P("role", SHARD),
            P(SHARD, None),
            P(None, SHARD),
            P(SHARD, "role"),
            P(SHARD, "role"),
            P("role", SHARD),
            P("role", SHARD),
        ),
        check_vma=False,
    )
```

profile of v0, /device:TPU:1, one launch (start us, length us, event | category | flops | bytes accessed | tf_op | source)
XLA Modules:
  0.0 454.9 jit_solution(15772133362649524636)
XLA Ops:
  8.6 68.0 %all-gather.2 = s32[32,1,9]{2,1,0:T(1,128)S(1)} all-gather(s32[1,1,9]{2,1,0:T(1,128)S(1)} %add_bitcast_fusion), channel_id=1, replica_groups=mesh['role'=4,'shard_0'=4,'shard_1'=4,'shard_2'=2] {'shard_0','shard_1',..., dimensions={0}, use_global_device_ids=true | all-gather | bytes 1188 | tf_op jit(solution)/shard_map/all_gather | solution.py:24
  77.0 5.0 %fusion.56 = f32[256,6144]{1,0:T(8,128)} fusion(bf16[256,128]{1,0:T(8,128)(2,1)S(1)} %convolution_convert_fusion.1, bf16[128,6144]{1,0:T(8,128)(2,1)} %param.17), kind=kOutput, calls=%fused_computation.85 | convolution fusion | flops 402653184 | bytes 7929856 | tf_op jit(solution)/shard_map/dot_general | solution.py:179
  83.0 1.8 convolution_bitcast_fusion
  84.9 4.0 all-to-all-start.1
  89.0 18.1 %all-to-all-done.1 = f32[32,8,2048]{2,1,0:T(8,128)S(1)} async-done(((f32[32,8,2048]{2,1,0:T(8,128)}), f32[32,8,2048]{2,1,0:T(8,128)S(1)}, u32[]{:S(2)}, u32[]{:S(2)}) %all-to-all-start.1) | async-done | bytes 2097184 | tf_op jit(solution)/shard_map/all_to_all | solution.py:55
  107.3 150.2 %reduce-scatter.3.cloned.1.call-done = f32[8,6144]{1,0:T(8,128)} async-done(((f32[256,6144]{1,0:T(8,128)}), f32[8,6144]{1,0:T(8,128)}) %reduce-scatter.3.cloned.1.call-update) | async-done | bytes 196624 | tf_op jit(solution)/shard_map/reduce_scatter | solution.py:178
  260.6 5.9 %all_gather.19 = bf16[2,8,6144]{2,1,0:T(8,128)(2,1)S(1)} all-gather(bf16[1,8,6144]{2,1,0:T(8,128)(2,1)S(1)} %pad_maximum_fusion.1), channel_id=1, replica_groups=mesh['role'=4,'shard_0'=4,'shard_1'=4,'shard_2'=2] {'shard_2'}, dimensions={0}, use_global_device_ids=true | all-gather | bytes 294912 | tf_op jit(solution)/shard_map/all_gather | solution.py:62
  266.5 11.7 %all-gather = bf16[8,8,6144]{2,1,0:T(8,128)(2,1)} all-gather(bf16[2,8,6144]{2,1,0:T(8,128)(2,1)S(1)} %all_gather.19), channel_id=2, replica_groups=mesh['role'=4,'shard_0'=4,'shard_1'=4,'shard_2'=2] {'shard_0'}, dimensions={0}, use_global_device_ids=true | all-gather | bytes 983040 | tf_op jit(solution)/shard_map/all_gather | solution.py:62
  279.6 3.9 all-to-all-start
  283.6 12.5 %all-to-all-done = bf16[32,8,2048]{2,1,0:T(8,128)(2,1)S(1)} async-done(((bf16[32,8,2048]{2,1,0:T(8,128)(2,1)}), bf16[32,8,2048]{2,1,0:T(8,128)(2,1)S(1)}, u32[]{:S(2)}, u32[]{:S(2)}) %all-to-all-start) | async-done | bytes 1048608 | tf_op jit(solution)/shard_map/all_to_all | solution.py:34
  297.6 52.3 %all-gather.5.cloned.1.call-done = bf16[16,2,8,6144]{3,2,1,0:T(8,128)(2,1)} async-done(((bf16[4,2,8,6144]{3,2,1,0:T(8,128)(2,1)}), bf16[16,2,8,6144]{3,2,1,0:T(8,128)(2,1)}) %all-gather.5.cloned.1.call-update) | async-done | bytes 3145744 | tf_op jit(solution)/shard_map/all_gather | solution.py:62
  349.9 2.2 copy.47
  352.8 2.1 reshape.319
  354.9 4.1 pad_maximum_fusion
  359.0 3.4 reshape.321
  362.4 38.6 %reduce-scatter.5.cloned.1.call-done = bf16[2048,128]{1,0:T(8,128)(2,1)} async-done(((bf16[8192,128]{1,0:T(8,128)(2,1)}), bf16[2048,128]{1,0:T(8,128)(2,1)}) %reduce-scatter.5.cloned.1.call-update) | async-done | bytes 524304 | tf_op jit(solution)/shard_map/reduce_scatter | solution.py:79
  402.2 2.0 fusion.31
  405.1 4.1 all-to-all-start.3
  409.2 3.2 fusion.22
  412.4 6.2 %all-to-all-done.3 = bf16[4,512,128]{2,1,0:T(8,128)(2,1)S(1)} async-done(((bf16[4,512,128]{2,1,0:T(8,128)(2,1)}), bf16[4,512,128]{2,1,0:T(8,128)(2,1)S(1)}, u32[]{:S(2)}, u32[]{:S(2)}) %all-to-all-start.3) | async-done | bytes 524320 | tf_op jit(solution)/shard_map/all_to_all | solution.py:34
  418.7 1.3 broadcast_in_dim.57
  420.0 4.4 all-to-all-start.2
  425.5 19.7 %all-to-all-done.2 = bf16[4,128,1536]{2,1,0:T(8,128)(2,1)S(1)} async-done(((bf16[4,128,1536]{2,1,0:T(8,128)(2,1)}), bf16[4,128,1536]{2,1,0:T(8,128)(2,1)S(1)}, u32[]{:S(2)}, u32[]{:S(2)}) %all-to-all-start.2) | async-done | bytes 1572896 | tf_op jit(solution)/shard_map/all_to_all | solution.py:34
  446.0 1.6 copy.49
  (59 shorter events, 13.8 us)
Async XLA Ops:
  7.2 69.6 %copy-start = (bf16[256,128]{1,0:T(8,128)(2,1)S(1)}, bf16[256,128]{1,0:T(8,128)(2,1)}, u32[]{:S(2)}) copy-start(bf16[256,128]{1,0:T(8,128)(2,1)} %param.14) | copy-start | bytes 196612
  7.2 250.3 %reduce-scatter.3.cloned.1.call-start = ((), (), s32[]{:S(2)}) async-start(), calls=%async_computation.6 | async-start | bytes 6488064 | tf_op jit(solution)/shard_map/reduce_scatter | solution.py:178
  82.0 1.0 copy-start.1
  82.0 1.0 copy-start.8
  84.9 22.3 %all-to-all-start.1 = ((f32[32,8,2048]{2,1,0:T(8,128)}), f32[32,8,2048]{2,1,0:T(8,128)S(1)}, u32[]{:S(2)}, u32[]{:S(2)}) async-start(f32[32,8,2048]{2,1,0:T(8,128)} %convolution_bitcast_fusion), calls=%async_computation.2 | async-start | bytes 4194304 | tf_op jit(solution)/shard_map/all_to_all | solution.py:55
  88.9 169.5 %copy-start.5 = (bf16[1,128,2048]{2,1,0:T(8,128)(2,1)S(1)}, bf16[1,128,2048]{2,1,0:T(8,128)(2,1)}, u32[]{:S(2)}) copy-start(bf16[1,128,2048]{2,1,0:T(8,128)(2,1)} %param.16) | copy-start | bytes 1572868
  88.9 169.5 %copy-start.6 = (bf16[1,128,2048]{2,1,0:T(8,128)(2,1)S(1)}, bf16[1,128,2048]{2,1,0:T(8,128)(2,1)}, u32[]{:S(2)}) copy-start(bf16[1,128,2048]{2,1,0:T(8,128)(2,1)} %param.15) | copy-start | bytes 1572868
  88.9 261.0 %all-gather.5.cloned.1.call-start = ((), (), s32[]{:S(2)}) async-start(), calls=%async_computation.8 | async-start | bytes 3932160 | tf_op jit(solution)/shard_map/all_gather | solution.py:62
  279.6 16.5 %all-to-all-start = ((bf16[32,8,2048]{2,1,0:T(8,128)(2,1)}), bf16[32,8,2048]{2,1,0:T(8,128)(2,1)S(1)}, u32[]{:S(2)}, u32[]{:S(2)}) async-start(bf16[32,8,2048]{2,1,0:T(8,128)(2,1)} %broadcast_in_dim.52), calls=%async_computation.1 | async-start | bytes 2097152 | tf_op jit(solution)/shard_map/all_to_all | solution.py:34
  283.5 117.5 %reduce-scatter.5.cloned.1.call-start = ((), (), s32[]{:S(2)}) async-start(), calls=%async_computation.7 | async-start | bytes 2621440 | tf_op jit(solution)/shard_map/reduce_scatter | solution.py:79
  362.4 39.8 %copy-start.2 = (bf16[2048,128]{1,0:T(8,128)(2,1)S(1)}, bf16[2048,128]{1,0:T(8,128)(2,1)}, u32[]{:S(2)}) copy-start(bf16[2048,128]{1,0:T(8,128)(2,1)} %param.18) | copy-start | bytes 1572868
  362.4 39.8 %copy-start.7 = (f32[512,128]{1,0:T(8,128)S(1)}, f32[512,128]{1,0:T(8,128)}, u32[]{:S(2)}) copy-start(f32[512,128]{1,0:T(8,128)} %param.21) | copy-start | bytes 786436
  405.1 13.6 %all-to-all-start.3 = ((bf16[4,512,128]{2,1,0:T(8,128)(2,1)}), bf16[4,512,128]{2,1,0:T(8,128)(2,1)S(1)}, u32[]{:S(2)}, u32[]{:S(2)}) async-start(bf16[4,512,128]{2,1,0:T(8,128)(2,1)} %broadcast_in_dim.58), calls=%async_computation.5 | async-start | bytes 1048576 | tf_op jit(solution)/shard_map/all_to_all | solution.py:34
  418.7 1.3 copy-start.3
  420.0 25.1 %all-to-all-start.2 = ((bf16[4,128,1536]{2,1,0:T(8,128)(2,1)}), bf16[4,128,1536]{2,1,0:T(8,128)(2,1)S(1)}, u32[]{:S(2)}, u32[]{:S(2)}) async-start(bf16[4,128,1536]{2,1,0:T(8,128)(2,1)} %broadcast_in_dim.57), calls=%async_computation.4 | async-start | bytes 3145728 | tf_op jit(solution)/shard_map/all_to_all | solution.py:34
  446.0 1.6 copy-start.4
Sparse Core Ops, SparseCore 0:
  82.2 175.2 reduce-scatter.2
  278.4 71.5 all-gather.4
  362.6 38.4 reduce-scatter.4
where the time goes:
time: 456 us; the launch traced here: 455 us
  waiting for transfers between devices  298 us (65%)
  blocking collectives  85.6 us (19%)
  local copies, waits for them, and re-layouts  16.7 us (4%)
  starting transfers between devices  16.6 us (4%)
  between operations  14.6 us (3%)
  other arithmetic  12.6 us (3%)
  matrix products  11.2 us (2%)
    reduce_scatter x1, waiting for transfers between devices, shards(): lax.psum_scatter(jnp.dot(inputs, qkv_weight, preferred_element_type=jnp.f...  150 us
    all_gather x1, blocking collectives, side_by_side(): lax.all_gather(both, axis, axis=dim, tiled=True)  68 us
    all_gather x1, waiting for transfers between devices, gather_in_order(): tiles = lax.all_gather(tiles, axes[k])  52.3 us
    reduce_scatter x1, waiting for transfers between devices, sum_packed(): lax.psum_scatter(lines, axis, tiled=True).reshape(-1)  38.6 us
    all_to_all x3, waiting for transfers between devices, from_everyone(): return lax.all_to_all(copies, axis, split_axis=0, concat_axis=0, tiled=True)  38.4 us
    all_to_all x1, waiting for transfers between devices, sent_and_summed(): lax.all_to_all(tiles, axis, split_axis=0, concat_axis=0, tiled=True)  18.1 us
    all_gather x2, blocking collectives, gather_in_order(): tiles = lax.all_gather(tiles, axes[k])  17.6 us
    all_to_all x3, starting transfers between devices, from_everyone(): return lax.all_to_all(copies, axis, split_axis=0, concat_axis=0, tiled=True)  12.4 us
  transfers between devices with their start and end apart: 7, of which 7 were waited for; matrix products, arithmetic and copies ran while one was open for 2% of the time, Pallas kernels for 0%

commit v1 on v0

v1 whole, which is shorter than its diff:
```python
import jax
import jax.numpy as jnp
from jax import lax
from jax.experimental import pallas as pl
from jax.experimental.pallas import tpu as pltpu
from jax.sharding import PartitionSpec as P

HD = 128
MESH = pl.DeviceIdType.MESH
F32 = jnp.float32
BF16 = jnp.bfloat16
LEARNER = 3

learn_rate = 0.001
first_decay = 0.9
second_decay = 0.95
adam_eps = 1e-08
weight_decay = 0.1
first_fix = 1.0 - 0.9**10
second_fix = 1.0 - 0.95**10
scale = HD ** (-0.5)

N_CHUNK = 4
CHUNK = 1536 // N_CHUNK


def adamw(params, gradient, first_moment, second_moment):
    moment_one = first_decay * first_moment + (1.0 - first_decay) * gradient
    moment_two = second_decay * second_moment + (1.0 - second_decay) * gradient * gradient
    stepped = moment_one / first_fix / (jnp.sqrt(moment_two / second_fix) + adam_eps)
    wide_params = params.astype(F32)
    updated = wide_params - learn_rate * (stepped + weight_decay * wide_params)
    return (updated, moment_one, moment_two)


def settle(ref, sem):
    pltpu.make_async_copy(ref, ref, sem).wait()


def nt(a, b):
    return lax.dot_general(a, b, (((1,), (1,)), ((), ())), preferred_element_type=F32)


def tn(a, b):
    return lax.dot_general(a, b, (((0,), (0,)), ((), ())), preferred_element_type=F32)


def nn(a, b):
    return jnp.dot(a, b, preferred_element_type=F32)


def kernel(
    ids_ref, len_ref, table_hbm, keys_hbm, vals_hbm, wqkv_hbm, wout_hbm,
    m_q_hbm, v_q_hbm, m_o_hbm, v_o_hbm, cot_hbm,
    dec_out, nq_out, no_out, mq_out, sq_out, mo_out, so_out,
    table, keys, vals, wq, wout, m_q, v_q, m_o, v_o, cot,
    tsend, trecv, gsend, grecv, idx4, idsend, idrecv, selsend, selrecv,
    xsend, xrecv, hrs, hrrecv, rsend, rmsg, agrecv, nq, no, dec,
    loc, out_sem, id_s, id_r, idg_s, idg_r, ts_s, ts_r, gs_s, gs_r,
    cot_s, cot_r, sel_s, sel_r, x_s, x_r, rel_s, rel_r, ag_s, ag_r, hr_s, hr_r,
    e_s, e_r,
):
    role = lax.axis_index("role")
    shard = lax.axis_index("shard")
    y, x, zl = shard // 8, (shard // 2) % 4, shard % 2
    z_hi, core = role // 2, role % 2
    sibling = z_hi * 2 + (1 - core)
    across = (1 - z_hi) * 2 + core

    def peer(k):
        py, px, pz = (y + k // 8) % 4, (x + (k // 2) % 4) % 4, (zl + k % 2) % 2
        spot = (px + py) % 4
        return py * 8 + px * 2 + pz, spot < 3, py * 6 + spot * 2 + pz

    my_spot = (x + y) % 4
    holder = my_spot < 3
    my_unit = jnp.where(holder, y * 6 + my_spot * 2 + zl, 0)

    def put(src, dst, send, recv, to_role, to_shard):
        pltpu.make_async_remote_copy(
            src_ref=src, dst_ref=dst, send_sem=send, recv_sem=recv,
            device_id=(to_role, to_shard), device_id_type=MESH,
        ).start()

    def each_peer(body):
        def step(k, carry):
            body(k, *peer(k))
            return carry
        lax.fori_loop(1, 32, step, 0)

    barrier = pltpu.get_barrier_semaphore()
    each_peer(lambda k, p, h, u: pl.semaphore_signal(
        barrier, inc=1, device_id=(role, p), device_id_type=MESH))
    for q in range(1, 4):
        pl.semaphore_signal(
            barrier, inc=1, device_id=((role + q) % 4, shard), device_id_type=MESH)

    col0 = pl.multiple_of(role * 1536, 128)
    row0 = pl.multiple_of(role * 512, 128)
    fetches = [
        pltpu.make_async_copy(a, b, loc.at[i])
        for i, (a, b) in enumerate((
            (table_hbm, table),
            (wqkv_hbm.at[:, pl.ds(col0, 1536)], wq),
            (wout_hbm, wout),
            (cot_hbm, cot),
            (keys_hbm.at[0], keys),
            (vals_hbm.at[0], vals),
            (m_q_hbm, m_q),
            (v_q_hbm, v_q),
            (m_o_hbm, m_o),
            (v_o_hbm, v_o),
        ))
    ]
    for i, f in enumerate(fetches):
        if i != 3:
            f.start()

    @pl.when(role == LEARNER)
    def _():
        fetches[3].start()

    row8 = lax.broadcasted_iota(jnp.int32, (8, 128), 0)
    lane8 = lax.broadcasted_iota(jnp.int32, (8, 128), 1)
    ids = jnp.zeros((8, 128), jnp.int32)
    for i in range(8):
        ids = jnp.where(row8 == i, ids_ref[0, i], ids)
    ids = ids.astype(F32)
    length = len_ref[0]
    live8 = row8 < length
    idx4[role] = ids

    fetches[0].wait()
    fetches[1].wait()
    for c in range(12):
        part = nn(table[...], wq[:, c * 128:(c + 1) * 128]).astype(BF16)
        tsend[2 * c] = part[0:128]
        tsend[2 * c + 1] = part[128:256]

    pl.semaphore_wait(barrier, 34)

    for q in range(1, 4):
        put(idx4.at[role], idx4.at[role], id_s.at[q - 1], id_r.at[q - 1], (role + q) % 4, shard)

    def send_part(k, p, h, u):
        @pl.when(h)
        def _():
            put(tsend.at[u], trecv.at[k - 1], ts_s, ts_r, role, p)
    each_peer(send_part)

    for q in range(1, 4):
        settle(idx4.at[0], id_r.at[q - 1])
    all_ids = jnp.concatenate([idx4[q] for q in range(4)], axis=0).astype(BF16)
    idsend[...] = all_ids
    idrecv[shard] = all_ids

    def send_ids(k, p, h, u):
        @pl.when(h)
        def _():
            put(idsend, idrecv.at[shard], idg_s, idg_r, role, p)
    each_peer(send_ids)

    fetches[2].wait()

    @pl.when(role == LEARNER)
    def _():
        fetches[3].wait()
        for q in range(3):
            put(cot_hbm, cot, cot_s.at[q], cot_r, q, shard)
        for i in range(8):
            upper = nt(cot[...], wout[i * 128:(i + 1) * 128, :]).reshape(32, 8, 128)
            lower = nt(cot[...], wout[1024 + i * 128:1024 + (i + 1) * 128, :]).reshape(32, 8, 128)
            gsend[:, :, i * 128:(i + 1) * 128] = jnp.concatenate([upper, lower], axis=1).astype(BF16)

        def send_grad(k, p, h, u):
            put(gsend.at[p], grecv.at[k - 1], gs_s, gs_r, role, p)
        each_peer(send_grad)

    @pl.when(holder)
    def _():
        settle(trecv, ts_r)

        def add(k, total):
            return total + trecv[k].astype(F32)
        total = lax.fori_loop(0, 31, add, tsend[my_unit].astype(F32))
        whole = total.astype(BF16)
        settle(idrecv.at[0:31], idg_r)
        lane = lax.broadcasted_iota(jnp.int32, (1024, 128), 1) + 128 * (my_unit % 2)
        chosen = jnp.where(
            idrecv[...].reshape(1024, 128).astype(F32) == lane.astype(F32), 1.0, 0.0).astype(BF16)
        selsend[...] = nn(chosen, whole).astype(BF16).reshape(32, 32, 128)

        def send_rows(k, p, h, u):
            put(selsend.at[p], selrecv.at[my_unit], sel_s, sel_r, role, p)
        each_peer(send_rows)
        selrecv[my_unit] = selsend[shard]
        settle(selrecv.at[0:23], sel_r)

    @pl.when(jnp.logical_not(holder))
    def _():
        settle(selrecv, sel_r)

    blocks = [selrecv[2 * c].astype(F32) + selrecv[2 * c + 1].astype(F32) for c in range(12)]
    for q in range(4):
        for i in range(6):
            pair = jnp.concatenate(
                [blocks[i][8 * q:8 * q + 8], blocks[6 + i][8 * q:8 * q + 8]], axis=0)
            xsend[q, :, i * 128:(i + 1) * 128] = pair.astype(BF16)
    for q in range(1, 4):
        to = (role + q) % 4
        put(xsend.at[to], xrecv.at[role], x_s.at[q - 1], x_r.at[q - 1], to, shard)
    xrecv[role] = xsend[role]
    fetches[4].wait()
    fetches[5].wait()
    for q in range(1, 4):
        settle(xrecv.at[0], x_r.at[q - 1])

    pieces = [xrecv[q].astype(F32) for q in range(4)]

    def tile(c):
        block, i = divmod(c, 12)
        return pieces[block][8 * (i // 6):8 * (i // 6) + 8, (i % 6) * 128:(i % 6 + 1) * 128]

    def stack(tiles):
        return jnp.concatenate(tiles, axis=0)

    q_tiles = [tile(h) for h in range(16)]
    q_all = stack(q_tiles).astype(BF16)
    k_new = stack([tile(16 + h) for h in range(16)]).astype(BF16)
    v_new = stack([tile(32 + h) for h in range(16)]).astype(BF16)

    def head(ref, h):
        return ref[:, h * 128:(h + 1) * 128]

    s1 = stack([nt(q_tiles[h].astype(BF16), head(keys, h)) for h in range(16)]) * scale
    s2 = nt(q_all, k_new) * scale
    ri = lax.broadcasted_iota(jnp.int32, (128, 128), 0)
    ci = lax.broadcasted_iota(jnp.int32, (128, 128), 1)
    allowed = (ri // 8 == ci // 8) & (ci % 8 <= ri % 8) & (ci % 8 < length)
    s2 = jnp.where(allowed, s2, -1e30)
    top = jnp.maximum(jnp.max(s1, axis=1, keepdims=True), jnp.max(s2, axis=1, keepdims=True))
    e1, e2 = jnp.exp(s1 - top), jnp.exp(s2 - top)
    den = jnp.sum(e1, axis=1, keepdims=True) + jnp.sum(e2, axis=1, keepdims=True)
    w1, w2 = e1 / den, e2 / den
    r2 = w2.astype(BF16)
    o2 = nn(r2, v_new)
    out_tiles = [
        nn(w1[8 * h:8 * h + 8].astype(BF16), head(vals, h)) + o2[8 * h:8 * h + 8]
        for h in range(16)
    ]
    for i in range(8):
        hrs[:, i * 128:(i + 1) * 128] = stack([out_tiles[i], out_tiles[8 + i]]).astype(BF16)

    @pl.when(role == LEARNER)
    def _():
        settle(grecv, gs_r)
        live16 = jnp.concatenate([live8, live8], axis=0)
        g_pieces = []
        for i in range(8):
            cols = slice(i * 128, (i + 1) * 128)

            def add(k, total):
                return total + grecv[k, :, cols].astype(F32)
            total = lax.fori_loop(0, 31, add, gsend[shard, :, cols].astype(F32), unroll=True)
            g_pieces.append(jnp.where(live16, total, 0.0))
        g_tiles = [g_pieces[h % 8][8 * (h // 8):8 * (h // 8) + 8] for h in range(16)]
        g_all = stack(g_tiles).astype(BF16)
        gw1 = stack([nt(g_tiles[h].astype(BF16), head(vals, h)) for h in range(16)])
        gw2 = nt(g_all, v_new)
        dots = jnp.sum(w1 * gw1, axis=1, keepdims=True) + jnp.sum(w2 * gw2, axis=1, keepdims=True)
        gs1 = w1 * (gw1 - dots) * scale
        gs2 = (w2 * (gw2 - dots) * scale).astype(BF16)
        gq2 = nn(gs2, k_new)
        gk = tn(gs2, q_all)
        gv = tn(r2, g_all)
        gp = [
            nn(gs1[8 * h:8 * h + 8].astype(BF16), head(keys, h)) + gq2[8 * h:8 * h + 8]
            for h in range(16)
        ]
        gp += [gk[8 * h:8 * h + 8] for h in range(16)]
        gp += [gv[8 * h:8 * h + 8] for h in range(16)]
        live_out = [jnp.where(live8, t, 0.0) for t in out_tiles]
        for q in range(4):
            tiles = [(gp[12 * q + i], gp[12 * q + 6 + i]) for i in range(6)]
            tiles += [(live_out[4 * q + i], live_out[4 * q + 2 + i]) for i in range(2)]
            tiles += [(ids, ids)]
            for i, pair in enumerate(tiles):
                rsend[q, :, i * 128:(i + 1) * 128] = stack(pair).astype(BF16)
        for q in range(3):
            put(rsend.at[q], rmsg, rel_s.at[q], rel_r, q, shard)
        rmsg[...] = rsend[3]

    @pl.when(role != LEARNER)
    def _():
        settle(rmsg, rel_r)
        settle(cot, cot_r)

    agrecv[shard] = rmsg[...]
    hrrecv[shard] = hrs[...]
    each_peer(lambda k, p, h, u: put(rmsg, agrecv.at[shard], ag_s, ag_r, role, p))
    each_peer(lambda k, p, h, u: put(hrs, hrrecv.at[shard], hr_s, hr_r, role, p))

    settle(agrecv.at[0:31], ag_r)
    got_ids = agrecv[:, :, 1024:1152].reshape(512, 128).astype(F32)
    lane = lax.broadcasted_iota(jnp.int32, (512, 128), 1).astype(F32)
    half = (lax.broadcasted_iota(jnp.int32, (512, 128), 0) // 8) % 2
    low = jnp.where(got_ids == lane, 1.0, 0.0).astype(BF16)
    high = jnp.where(got_ids == lane + 128.0, 1.0, 0.0).astype(BF16)
    rows = nn(low, table[0:128, :]) + nn(high, table[128:256, :])
    halves = [jnp.where(half == j, rows, 0.0).astype(BF16) for j in range(2)]
    for f in fetches[6:]:
        f.wait()

    copies = []

    def copy_out(a, b):
        c = pltpu.make_async_copy(a, b, out_sem.at[len(copies)])
        c.start()
        copies.append(c)

    def spread(src, dst, n):
        put(src, dst, e_s.at[0, n], e_r.at[0, n], sibling, shard)
        put(src, dst, e_s.at[1, n], e_r.at[1, n], across, shard)
        copy_out(src, dst)

    def q_cols(of, c):
        return nq_out.at[:, pl.ds(pl.multiple_of(of * 1536 + c * CHUNK, 128), CHUNK)]

    def o_rows(of):
        return no_out.at[pl.ds(pl.multiple_of(of * 512, 128), 512), :]

    for c in range(N_CHUNK):
        j, at = divmod(c * CHUNK, 768)
        cols = slice(c * CHUNK, (c + 1) * CHUNK)
        grad = tn(halves[j], agrecv[:, :, at:at + CHUNK].reshape(512, CHUNK))
        new, one, two = adamw(wq[:, cols], grad, m_q[:, cols], v_q[:, cols])
        nq[:, cols] = new.astype(BF16)
        m_q[:, cols] = one
        v_q[:, cols] = two
        spread(nq.at[:, cols], q_cols(role, c), c)

    cot_wide = jnp.broadcast_to(
        cot[...].astype(F32).reshape(32, 1, 8, 128), (32, 2, 8, 128)).reshape(512, 128)
    cot_both = jnp.concatenate(
        [jnp.where(half == j, cot_wide, 0.0).astype(BF16) for j in range(2)], axis=1)
    grad_out = tn(agrecv[:, :, 768:1024].reshape(512, 256), cot_both)
    for j in range(2):
        here = slice(j * 256, (j + 1) * 256)
        params = wout[pl.ds(pl.multiple_of(row0 + j * 256, 128), 256), :]
        new, one, two = adamw(
            params, grad_out[:, j * 128:(j + 1) * 128], m_o[here, :], v_o[here, :])
        no[here, :] = new.astype(BF16)
        m_o[here, :] = one
        v_o[here, :] = two
    spread(no, o_rows(role), N_CHUNK)
    copy_out(m_q, mq_out)
    copy_out(v_q, sq_out)
    copy_out(m_o, mo_out)
    copy_out(v_o, so_out)

    def part(of, n):
        return q_cols(of, n) if n < N_CHUNK else o_rows(of)

    for n in range(N_CHUNK + 1):
        settle(part(across, n), e_r.at[1, n])
        put(part(across, n), part(across, n), e_s.at[2, n], e_r.at[2, n], sibling, shard)

    settle(hrrecv.at[0:31], hr_r)
    mix = hrrecv[...].reshape(512, 1024)
    upper = nn(mix, wout[0:1024, :]).reshape(32, 2, 8, 128)
    lower = nn(mix, wout[1024:2048, :]).reshape(32, 2, 8, 128)
    dec[...] = (upper[:, 0] + lower[:, 1]).reshape(256, 128).astype(BF16)
    copy_out(dec, dec_out)

    for n in range(N_CHUNK + 1):
        settle(part(sibling, n), e_r.at[0, n])
        settle(part((1 - z_hi) * 2 + (1 - core), n), e_r.at[2, n])
        for way in range(3):
            settle(part(role, n), e_s.at[way, n])
    for c in copies:
        c.wait()
    for q in range(3):
        settle(idx4.at[0], id_s.at[q])
        settle(xsend.at[0], x_s.at[q])

    @pl.when(holder)
    def _():
        settle(tsend.at[0:23], ts_s)
        settle(idrecv.at[0:23], idg_s)
        settle(selsend.at[0:31], sel_s)

    @pl.when(jnp.logical_not(holder))
    def _():
        settle(tsend, ts_s)
        settle(idrecv.at[0:24], idg_s)

    @pl.when(role == LEARNER)
    def _():
        settle(gsend.at[0:31], gs_s)
        for q in range(3):
            settle(cot, cot_s.at[q])
            settle(rmsg, rel_s.at[q])
    settle(agrecv.at[0:31], ag_s)
    settle(hrrecv.at[0:31], hr_s)


def shards(*args):
    any_ = pl.BlockSpec(memory_space=pl.ANY)
    smem = pl.BlockSpec(memory_space=pltpu.SMEM)
    dma, vm = pltpu.SemaphoreType.DMA, pltpu.VMEM
    return tuple(pl.pallas_call(
        kernel,
        out_shape=(
            jax.ShapeDtypeStruct((256, 128), BF16),
            jax.ShapeDtypeStruct((128, 6144), BF16),
            jax.ShapeDtypeStruct((2048, 128), BF16),
            jax.ShapeDtypeStruct((128, 1536), F32),
            jax.ShapeDtypeStruct((128, 1536), F32),
            jax.ShapeDtypeStruct((512, 128), F32),
            jax.ShapeDtypeStruct((512, 128), F32),
        ),
        in_specs=[smem, smem] + [any_] * 10,
        out_specs=(any_,) * 7,
        scratch_shapes=[
            vm((256, 128), BF16),
            vm((128, 2048), BF16),
            vm((128, 2048), BF16),
            vm((128, 1536), BF16),
            vm((2048, 128), BF16),
            vm((128, 1536), F32),
            vm((128, 1536), F32),
            vm((512, 128), F32),
            vm((512, 128), F32),
            vm((256, 128), BF16),
            vm((24, 128, 128), BF16),
            vm((31, 128, 128), BF16),
            vm((32, 16, 1024), BF16),
            vm((31, 16, 1024), BF16),
            vm((4, 8, 128), F32),
            vm((32, 128), BF16),
            vm((32, 32, 128), BF16),
            vm((32, 32, 128), BF16),
            vm((24, 32, 128), BF16),
            vm((4, 16, 768), BF16),
            vm((4, 16, 768), BF16),
            vm((16, 1024), BF16),
            vm((32, 16, 1024), BF16),
            vm((4, 16, 1152), BF16),
            vm((16, 1152), BF16),
            vm((32, 16, 1152), BF16),
            vm((128, 1536), BF16),
            vm((512, 128), BF16),
            vm((256, 128), BF16),
            dma((10,)),
            dma((N_CHUNK + 6,)),
            dma((3,)), dma((3,)),
            dma, dma,
            dma, dma,
            dma, dma,
            dma((3,)), dma,
            dma, dma,
            dma((3,)), dma((3,)),
            dma((3,)), dma,
            dma, dma,
            dma, dma,
            dma((3, N_CHUNK + 1)), dma((3, N_CHUNK + 1)),
        ],
        compiler_params=pltpu.CompilerParams(
            collective_id=0, has_side_effects=True, vmem_limit_bytes=48 * 1024 * 1024),
        name="policy_update",
    )(*args))


def solution(mesh):
    both = ("role", "shard")
    return jax.shard_map(
        shards,
        mesh=mesh,
        in_specs=(
            P(both, None), P(both), P(None, "shard"), P(both, None, None), P(both, None, None),
            P("shard", None), P(None, "shard"), P("shard", "role"), P("shard", "role"),
            P("role", "shard"), P("role", "shard"), P("role", "shard"),
        ),
        out_specs=(
            P("role", "shard"), P("shard", None), P(None, "shard"), P("shard", "role"),
            P("shard", "role"), P("role", "shard"), P("role", "shard"),
        ),
        check_vma=False,
    )
```

time: 456 us -> 109 us (0.24)
  waiting for transfers between devices: 298 us -> 0 us
  Pallas kernels: 0 us -> 89.8 us
  blocking collectives: 85.6 us -> 0 us
  starting transfers between devices: 16.6 us -> 0 us
  between operations: 14.6 us -> 1.31 us
  other arithmetic: 12.6 us -> 0 us
  matrix products: 11.2 us -> 0 us
    reduce_scatter x2 -> x0, waiting for transfers between devices: 189 us -> none  [the longest x1 150 us: shards(): lax.psum_scatter(jnp.dot(inputs, qkv_weight, preferred_element_type=jnp.f...]
    pallas_call x0 -> x1, Pallas kernels: none -> 89.8 us  [shards(): pl.pallas_call(kernel, out_shape=(jax.ShapeDtypeStruct((256, 128), BF16),...]
    all_gather x3 -> x0, blocking collectives: 85.6 us -> none  [the longest x1 68 us: side_by_side(): lax.all_gather(both, axis, axis=dim, tiled=True)]
    all_to_all x4 -> x0, waiting for transfers between devices: 56.5 us -> none  [the longest x3 38.4 us: from_everyone(): return lax.all_to_all(copies, axis, split_axis=0, concat_axis=0, tiled=True)]
    all_gather x1 -> x0, waiting for transfers between devices: 52.3 us -> none  [gather_in_order(): tiles = lax.all_gather(tiles, axes[k])]
    all_to_all x4 -> x0, starting transfers between devices: 16.5 us -> none  [the longest x3 12.4 us: from_everyone(): return lax.all_to_all(copies, axis, split_axis=0, concat_axis=0, tiled=True)]
    unnamed x22 -> x25, local copies, waits for them, and re-layouts: 3.3 us -> 15.8 us
    dot_general x11 -> x0, matrix products: 10.6 us -> none  [the longest x1 5.04 us: shards(): jnp.dot(inputs, qkv_weight, preferred_element_type=jnp.float32)]
  transfers between devices with their start and end apart: 7 -> 0, of which waited for: 7 -> 0; matrix products, arithmetic and copies ran while one was open for 2% -> 0% of each run, Pallas kernels for 0% -> 0%
where the time goes in v1:
time: 109 us; the launch traced here: 107 us
  Pallas kernels  89.8 us (82%)
  local copies, waits for them, and re-layouts  15.8 us (14%)
  between operations  1.31 us (1%)
    pallas_call x1, Pallas kernels, shards(): pl.pallas_call(kernel, out_shape=(jax.ShapeDtypeStruct((256, 128), BF16),...  89.8 us
    unnamed x25, local copies, waits for them, and re-layouts  15.8 us

profile of v1, /device:TPU:1, one launch (start us, length us, event | category | flops | bytes accessed | tf_op | source)
XLA Modules:
  0.0 106.8 jit_solution(8339787564693294927)
XLA Ops:
  1.3 0.0 copy-start
  1.3 1.1 %copy-done = f32[128,1536]{1,0:T(8,128)S(1)} copy-done((f32[128,1536]{1,0:T(8,128)S(1)}, f32[128,1536]{1,0:T(8,128)}, u32[]{:S(2)}) %copy-start) | copy-done | bytes 786456
  2.4 0.0 copy-start.1
  2.4 1.0 copy-done.1
  3.5 0.0 copy-start.2
  3.5 1.0 copy-done.2
  4.5 0.0 copy-start.3
  4.5 1.0 copy-done.3
  5.5 0.0 copy-start.4
  5.5 0.9 copy-done.4
  6.5 0.0 copy-start.5
  6.5 0.9 copy-done.5
  7.4 0.0 copy-start.6
  7.4 0.8 copy-done.6
  8.3 0.8 copy-done.7
  9.1 0.7 copy-done.8
  9.8 89.8 %policy_update.1 = (bf16[256,128]{1,0:T(8,128)(2,1)S(1)}, bf16[128,6144]{1,0:T(8,128)(2,1)}, bf16[2048,128]{1,0:T(8,128)(2,1)S(1)}, f32[128,1536]{1,0:T(8,128)S(...) custom-call(s32[1,8]{1,0:T(1,128)S(1)} %copy-done.8, s32[1]{0:T(128)S(6)} %copy.26.len_ref, ...), custom_call_target="tpu_custom_call" | custom-call | tf_op jit(solution)/shard_map/policy_update/pallas_call | solution.py:411
  99.5 0.6 copy.27
  100.2 2.7 %copy.28 = bf16[128,6144]{1,0:T(8,128)(2,1)} copy(bf16[128,6144]{1,0:T(8,128)(2,1)} %get-tuple-element.15) | data formatting | bytes 3145728
  102.9 0.8 copy.29
  103.7 0.9 copy.30
  104.5 0.9 copy.31
  105.4 0.7 copy.32
  106.1 0.7 copy.33
  (2 shorter events, 0.0 us)
Async XLA Ops:
  1.3 1.1 %copy-start = (f32[128,1536]{1,0:T(8,128)S(1)}, f32[128,1536]{1,0:T(8,128)}, u32[]{:S(2)}) copy-start(f32[128,1536]{1,0:T(8,128)} %m_q_hbm.1) | copy-start | bytes 2359300
  2.4 1.0 copy-start.1
  3.5 1.0 copy-start.2
  4.5 1.0 copy-start.3
  5.5 0.9 copy-start.4
  6.5 0.9 copy-start.5
  7.4 0.8 copy-start.6
  8.3 0.8 copy-start.7
  9.1 0.7 copy-start.8

commit v2 on v1

--- a/solution.py
+++ b/solution.py
@@ -21,6 +21,7 @@
 scale = HD ** (-0.5)
 
 N_CHUNK = 4
+ORDER = 13
 CHUNK = 1536 // N_CHUNK
 
 
@@ -82,11 +83,12 @@
             device_id=(to_role, to_shard), device_id_type=MESH,
         ).start()
 
-    def each_peer(body):
-        def step(k, carry):
+    def each_peer(body, first=1, last=32):
+        def step(j, carry):
+            k = (j * ORDER) % 32
             body(k, *peer(k))
             return carry
-        lax.fori_loop(1, 32, step, 0)
+        lax.fori_loop(first, last, step, 0)
 
     barrier = pltpu.get_barrier_semaphore()
     each_peer(lambda k, p, h, u: pl.semaphore_signal(
@@ -146,35 +148,43 @@
         @pl.when(h)
         def _():
             put(tsend.at[u], trecv.at[k - 1], ts_s, ts_r, role, p)
-    each_peer(send_part)
+    each_peer(send_part, 1, 12)
 
     for q in range(1, 4):
         settle(idx4.at[0], id_r.at[q - 1])
-    all_ids = jnp.concatenate([idx4[q] for q in range(4)], axis=0).astype(BF16)
+    lane16 = lax.broadcasted_iota(jnp.int32, (16, 128), 1)
+    all_ids = jnp.where(
+        lane16 < 64,
+        jnp.concatenate([idx4[0], idx4[1]], axis=0),
+        jnp.concatenate([idx4[2], idx4[3]], axis=0)).astype(BF16)
     idsend[...] = all_ids
     idrecv[shard] = all_ids
 
-    def send_ids(k, p, h, u):
-        @pl.when(h)
-        def _():
-            put(idsend, idrecv.at[shard], idg_s, idg_r, role, p)
-    each_peer(send_ids)
-
-    fetches[2].wait()
+    def send_ids(now):
+        def body(k, p, h, u):
+            @pl.when(h if now else jnp.logical_not(h))
+            def _():
+                put(idsend, idrecv.at[shard], idg_s, idg_r, role, p)
+        each_peer(body)
+    send_ids(True)
+    each_peer(send_part, 12, 32)
 
     @pl.when(role == LEARNER)
     def _():
+        fetches[2].wait()
         fetches[3].wait()
-        for q in range(3):
-            put(cot_hbm, cot, cot_s.at[q], cot_r, q, shard)
         for i in range(8):
-            upper = nt(cot[...], wout[i * 128:(i + 1) * 128, :]).reshape(32, 8, 128)
-            lower = nt(cot[...], wout[1024 + i * 128:1024 + (i + 1) * 128, :]).reshape(32, 8, 128)
-            gsend[:, :, i * 128:(i + 1) * 128] = jnp.concatenate([upper, lower], axis=1).astype(BF16)
-
-        def send_grad(k, p, h, u):
-            put(gsend.at[p], grecv.at[k - 1], gs_s, gs_r, role, p)
-        each_peer(send_grad)
+            upper, lower = (
+                nt(cot[...], wout[j * 1024 + i * 128:j * 1024 + (i + 1) * 128, :])
+                .reshape(32, 8, 128)
+                for j in range(2)
+            )
+            gsend[:, :, i * 128:(i + 1) * 128] = jnp.concatenate(
+                [upper, lower], axis=1).astype(BF16)
+
+    @pl.when(role != LEARNER)
+    def _():
+        fetches[2].wait()
 
     @pl.when(holder)
     def _():
@@ -185,19 +195,31 @@
         total = lax.fori_loop(0, 31, add, tsend[my_unit].astype(F32))
         whole = total.astype(BF16)
         settle(idrecv.at[0:31], idg_r)
+        got = idrecv[...].astype(F32)
+        got = jnp.concatenate([
+            jnp.broadcast_to(got[:, :, 0:1], (32, 16, 128)),
+            jnp.broadcast_to(got[:, :, 64:65], (32, 16, 128))], axis=1).reshape(1024, 128)
         lane = lax.broadcasted_iota(jnp.int32, (1024, 128), 1) + 128 * (my_unit % 2)
-        chosen = jnp.where(
-            idrecv[...].reshape(1024, 128).astype(F32) == lane.astype(F32), 1.0, 0.0).astype(BF16)
+        chosen = jnp.where(got == lane.astype(F32), 1.0, 0.0).astype(BF16)
         selsend[...] = nn(chosen, whole).astype(BF16).reshape(32, 32, 128)
 
         def send_rows(k, p, h, u):
             put(selsend.at[p], selrecv.at[my_unit], sel_s, sel_r, role, p)
         each_peer(send_rows)
         selrecv[my_unit] = selsend[shard]
+
+    @pl.when(role == LEARNER)
+    def _():
+        each_peer(lambda k, p, h, u: put(gsend.at[p], grecv.at[k - 1], gs_s, gs_r, role, p))
+    send_ids(False)
+
+    @pl.when(holder)
+    def _():
         settle(selrecv.at[0:23], sel_r)
 
     @pl.when(jnp.logical_not(holder))
     def _():
+        settle(idrecv.at[0:31], idg_r)
         settle(selrecv, sel_r)
 
     blocks = [selrecv[2 * c].astype(F32) + selrecv[2 * c + 1].astype(F32) for c in range(12)]
@@ -254,16 +276,14 @@
     @pl.when(role == LEARNER)
     def _():
         settle(grecv, gs_r)
-        live16 = jnp.concatenate([live8, live8], axis=0)
-        g_pieces = []
+        g_tiles = [None] * 16
         for i in range(8):
             cols = slice(i * 128, (i + 1) * 128)
-
-            def add(k, total):
-                return total + grecv[k, :, cols].astype(F32)
-            total = lax.fori_loop(0, 31, add, gsend[shard, :, cols].astype(F32), unroll=True)
-            g_pieces.append(jnp.where(live16, total, 0.0))
-        g_tiles = [g_pieces[h % 8][8 * (h // 8):8 * (h // 8) + 8] for h in range(16)]
+            total = gsend[shard, :, cols].astype(F32)
+            for k in range(31):
+                total += grecv[k, :, cols].astype(F32)
+            g_tiles[i] = jnp.where(live8, total[0:8], 0.0)
+            g_tiles[8 + i] = jnp.where(live8, total[8:16], 0.0)
         g_all = stack(g_tiles).astype(BF16)
         gw1 = stack([nt(g_tiles[h].astype(BF16), head(vals, h)) for h in range(16)])
         gw2 = nt(g_all, v_new)
@@ -283,25 +303,93 @@
         for q in range(4):
             tiles = [(gp[12 * q + i], gp[12 * q + 6 + i]) for i in range(6)]
             tiles += [(live_out[4 * q + i], live_out[4 * q + 2 + i]) for i in range(2)]
-            tiles += [(ids, ids)]
             for i, pair in enumerate(tiles):
                 rsend[q, :, i * 128:(i + 1) * 128] = stack(pair).astype(BF16)
         for q in range(3):
             put(rsend.at[q], rmsg, rel_s.at[q], rel_r, q, shard)
+        for q in range(3):
+            put(cot_hbm, cot, cot_s.at[q], cot_r, q, shard)
         rmsg[...] = rsend[3]
 
+    def shard_at(py, px, pz):
+        return (py % 4) * 8 + (px % 4) * 2 + pz % 2
+
+    class Gather:
+        def __init__(self, msg, buf, send, recv):
+            self.msg, self.buf, self.send, self.recv = msg, buf, send, recv
+
+        def hop(self, step, half, src, dst, dy, dx, dz):
+            put(src, dst, self.send, self.recv.at[half, step], role,
+                shard_at(y + dy, x + dx, zl + dz))
+
+        def first(self):
+            self.buf[y, x, zl] = self.msg[...]
+            for half in range(2):
+                lanes = pl.ds(half * 512, 512)
+                for d, dz in ((1, 0), (3, 0), (0, 1), (1, 1), (3, 1)):
+                    self.hop(0, half, self.msg.at[:, lanes], self.buf.at[y, x, zl, :, lanes],
+                             d * half, d * (1 - half), dz)
+
+        def second(self):
+            for half in range(2):
+                settle(selrecv.at[0:10], self.recv.at[half, 0])
+                lanes = pl.ds(half * 512, 512)
+                dy, dx = half, 1 - half
+                before = self.buf.at[(y + 3 * dy) % 4, (x + 3 * dx) % 4, zl, :, lanes]
+                after = self.buf.at[(y + dy) % 4, (x + dx) % 4, 1 - zl, :, lanes]
+                self.hop(1, half, before, before, dy, dx, 0)
+                self.hop(1, half, after, after, 3 * dy, 3 * dx, 0)
+
+        def third(self):
+            for half in range(2):
+                settle(trecv.at[0:1], self.recv.at[half, 1])
+                lanes = pl.ds(half * 512, 512)
+                line = self.buf.at[:, x, :, :, lanes] if half else self.buf.at[y, :, :, :, lanes]
+                for d in (1, 3):
+                    self.hop(2, half, line, line, d * (1 - half), d * half, 0)
+
+        def fourth(self):
+            for half in range(2):
+                settle(trecv.at[0:8], self.recv.at[half, 2])
+                lanes = pl.ds(half * 512, 512)
+                if half:
+                    before = self.buf.at[0:2, (x + 3) % 4, :, :, lanes]
+                    after = self.buf.at[2:4, (x + 1) % 4, :, :, lanes]
+                else:
+                    before = self.buf.at[(y + 3) % 4, 0:2, :, :, lanes]
+                    after = self.buf.at[(y + 1) % 4, 2:4, :, :, lanes]
+                self.hop(3, half, before, before, 1 - half, half, 0)
+                self.hop(3, half, after, after, 3 * (1 - half), 3 * half, 0)
+
+        def last(self):
+            for half in range(2):
+                settle(trecv.at[0:4], self.recv.at[half, 3])
+
+        def sent(self):
+            settle(trecv, self.send)
+
+    mixes = Gather(hrs, hrrecv, hr_s, hr_r)
+    grads = Gather(rmsg, agrecv, ag_s, ag_r)
+
     @pl.when(role != LEARNER)
     def _():
+        mixes.first()
         settle(rmsg, rel_r)
-        settle(cot, cot_r)
-
-    agrecv[shard] = rmsg[...]
-    hrrecv[shard] = hrs[...]
-    each_peer(lambda k, p, h, u: put(rmsg, agrecv.at[shard], ag_s, ag_r, role, p))
-    each_peer(lambda k, p, h, u: put(hrs, hrrecv.at[shard], hr_s, hr_r, role, p))
-
-    settle(agrecv.at[0:31], ag_r)
-    got_ids = agrecv[:, :, 1024:1152].reshape(512, 128).astype(F32)
+    grads.first()
+
+    @pl.when(role == LEARNER)
+    def _():
+        mixes.first()
+    grads.second()
+    grads.third()
+    mixes.second()
+    grads.fourth()
+    mixes.third()
+    grads.last()
+
+    got_ids = idrecv[...].astype(F32)[:, 8:16, 64:65]
+    got_ids = jnp.broadcast_to(
+        jnp.concatenate([got_ids, got_ids], axis=1), (32, 16, 128)).reshape(512, 128)
     lane = lax.broadcasted_iota(jnp.int32, (512, 128), 1).astype(F32)
     half = (lax.broadcasted_iota(jnp.int32, (512, 128), 0) // 8) % 2
     low = jnp.where(got_ids == lane, 1.0, 0.0).astype(BF16)
@@ -332,18 +420,21 @@
     for c in range(N_CHUNK):
         j, at = divmod(c * CHUNK, 768)
         cols = slice(c * CHUNK, (c + 1) * CHUNK)
-        grad = tn(halves[j], agrecv[:, :, at:at + CHUNK].reshape(512, CHUNK))
+        grad = tn(halves[j], agrecv[:, :, :, :, at:at + CHUNK].reshape(512, CHUNK))
         new, one, two = adamw(wq[:, cols], grad, m_q[:, cols], v_q[:, cols])
         nq[:, cols] = new.astype(BF16)
         m_q[:, cols] = one
         v_q[:, cols] = two
         spread(nq.at[:, cols], q_cols(role, c), c)
 
+    @pl.when(role != LEARNER)
+    def _():
+        settle(cot, cot_r)
     cot_wide = jnp.broadcast_to(
         cot[...].astype(F32).reshape(32, 1, 8, 128), (32, 2, 8, 128)).reshape(512, 128)
     cot_both = jnp.concatenate(
         [jnp.where(half == j, cot_wide, 0.0).astype(BF16) for j in range(2)], axis=1)
-    grad_out = tn(agrecv[:, :, 768:1024].reshape(512, 256), cot_both)
+    grad_out = tn(agrecv[:, :, :, :, 768:1024].reshape(512, 256), cot_both)
     for j in range(2):
         here = slice(j * 256, (j + 1) * 256)
         params = wout[pl.ds(pl.multiple_of(row0 + j * 256, 128), 256), :]
@@ -358,6 +449,8 @@
     copy_out(m_o, mo_out)
     copy_out(v_o, so_out)
 
+    mixes.fourth()
+
     def part(of, n):
         return q_cols(of, n) if n < N_CHUNK else o_rows(of)
 
@@ -365,7 +458,7 @@
         settle(part(across, n), e_r.at[1, n])
         put(part(across, n), part(across, n), e_s.at[2, n], e_r.at[2, n], sibling, shard)
 
-    settle(hrrecv.at[0:31], hr_r)
+    mixes.last()
     mix = hrrecv[...].reshape(512, 1024)
     upper = nn(mix, wout[0:1024, :]).reshape(32, 2, 8, 128)
     lower = nn(mix, wout[1024:2048, :]).reshape(32, 2, 8, 128)
@@ -386,39 +479,56 @@
     @pl.when(holder)
     def _():
         settle(tsend.at[0:23], ts_s)
-        settle(idrecv.at[0:23], idg_s)
         settle(selsend.at[0:31], sel_s)
 
     @pl.when(jnp.logical_not(holder))
     def _():
         settle(tsend, ts_s)
-        settle(idrecv.at[0:24], idg_s)
 
     @pl.when(role == LEARNER)
     def _():
-        settle(gsend.at[0:31], gs_s)
         for q in range(3):
             settle(cot, cot_s.at[q])
             settle(rmsg, rel_s.at[q])
-    settle(agrecv.at[0:31], ag_s)
-    settle(hrrecv.at[0:31], hr_s)
+        settle(gsend.at[0:31], gs_s)
+    settle(idrecv.at[0:31], idg_s)
+    grads.sent()
+    mixes.sent()
+
+
+SHAPES = (
+    ((256, 128), BF16), ((128, 6144), BF16), ((2048, 128), BF16),
+    ((128, 1536), F32), ((128, 1536), F32), ((512, 128), F32), ((512, 128), F32),
+)
+
+
+def hand_over(*refs):
+    ins, outs, stage, sems = refs[:7], refs[7:14], refs[14:21], refs[21]
+    moves = []
+    for a, v, b in zip(ins, stage, outs):
+        pieces = 4 if a.shape == (128, 6144) else 2 if a.shape[0] * a.shape[1] > 131072 else 1
+        rows = a.shape[0] // pieces
+        for i in range(pieces):
+            part, n = pl.ds(i * rows, rows), len(moves)
+            moves.append((
+                pltpu.make_async_copy(a.at[part, :], v.at[part, :], sems.at[0, n]),
+                pltpu.make_async_copy(v.at[part, :], b.at[part, :], sems.at[1, n])))
+    for m, _ in moves:
+        m.start()
+    for m, n in moves:
+        m.wait()
+        n.start()
+    for _, n in moves:
+        n.wait()
 
 
 def shards(*args):
     any_ = pl.BlockSpec(memory_space=pl.ANY)
     smem = pl.BlockSpec(memory_space=pltpu.SMEM)
     dma, vm = pltpu.SemaphoreType.DMA, pltpu.VMEM
-    return tuple(pl.pallas_call(
+    done = pl.pallas_call(
         kernel,
-        out_shape=(
-            jax.ShapeDtypeStruct((256, 128), BF16),
-            jax.ShapeDtypeStruct((128, 6144), BF16),
-            jax.ShapeDtypeStruct((2048, 128), BF16),
-            jax.ShapeDtypeStruct((128, 1536), F32),
-            jax.ShapeDtypeStruct((128, 1536), F32),
-            jax.ShapeDtypeStruct((512, 128), F32),
-            jax.ShapeDtypeStruct((512, 128), F32),
-        ),
+        out_shape=tuple(jax.ShapeDtypeStruct(*a) for a in SHAPES),
         in_specs=[smem, smem] + [any_] * 10,
         out_specs=(any_,) * 7,
         scratch_shapes=[
@@ -437,17 +547,17 @@
             vm((32, 16, 1024), BF16),
             vm((31, 16, 1024), BF16),
             vm((4, 8, 128), F32),
-            vm((32, 128), BF16),
-            vm((32, 32, 128), BF16),
+            vm((16, 128), BF16),
+            vm((32, 16, 128), BF16),
             vm((32, 32, 128), BF16),
             vm((24, 32, 128), BF16),
             vm((4, 16, 768), BF16),
             vm((4, 16, 768), BF16),
             vm((16, 1024), BF16),
-            vm((32, 16, 1024), BF16),
-            vm((4, 16, 1152), BF16),
-            vm((16, 1152), BF16),
-            vm((32, 16, 1152), BF16),
+            vm((4, 4, 2, 16, 1024), BF16),
+            vm((4, 16, 1024), BF16),
+            vm((16, 1024), BF16),
+            vm((4, 4, 2, 16, 1024), BF16),
             vm((128, 1536), BF16),
             vm((512, 128), BF16),
             vm((256, 128), BF16),
@@ -461,14 +571,23 @@
             dma, dma,
             dma((3,)), dma((3,)),
             dma((3,)), dma,
-            dma, dma,
-            dma, dma,
+            dma, dma((2, 4)),
+            dma, dma((2, 4)),
             dma((3, N_CHUNK + 1)), dma((3, N_CHUNK + 1)),
         ],
         compiler_params=pltpu.CompilerParams(
-            collective_id=0, has_side_effects=True, vmem_limit_bytes=48 * 1024 * 1024),
+            collective_id=0, has_side_effects=True, vmem_limit_bytes=60 * 1024 * 1024),
         name="policy_update",
-    )(*args))
+    )(*args)
+    return tuple(pl.pallas_call(
+        hand_over,
+        out_shape=tuple(jax.ShapeDtypeStruct(*a) for a in SHAPES),
+        in_specs=[any_] * 7,
+        out_specs=(any_,) * 7,
+        scratch_shapes=[vm(*a) for a in SHAPES] + [dma((2, 16))],
+        compiler_params=pltpu.CompilerParams(vmem_limit_bytes=60 * 1024 * 1024),
+        name="hand_over",
+    )(*done))
 
 
 def solution(mesh):

time: 109 us -> 81.6 us (0.75); the launches traced: 107 us -> 81.5 us
  local copies, waits for them, and re-layouts: 15.8 us -> 0 us
  Pallas kernels: 89.8 us -> 80.2 us
    unnamed x25 -> x0, local copies, waits for them, and re-layouts: 15.8 us -> none
    pallas_call x1 -> x2, Pallas kernels: 89.8 us -> 80.2 us  [the longest x1 76.4 us: shards(): pl.pallas_call(kernel, out_shape=tuple((jax.ShapeDtypeStruct(*a) for a in...]
where the time goes in v2:
time: 81.6 us; the launch traced here: 81.5 us
  Pallas kernels  80.2 us (98%)
  between operations  1.29 us (2%)
    pallas_call x1, Pallas kernels, shards(): pl.pallas_call(kernel, out_shape=tuple((jax.ShapeDtypeStruct(*a) for a in...  76.4 us
    pallas_call x1, Pallas kernels, shards(): pl.pallas_call(hand_over, out_shape=tuple((jax.ShapeDtypeStruct(*a) for a...  3.84 us

profile of v2, /device:TPU:1, one launch (start us, length us, event | category | flops | bytes accessed | tf_op | source)
XLA Modules:
  0.0 81.5 jit_solution(8900004059332774768)
XLA Ops:
  1.3 76.4 %policy_update.1 = (bf16[256,128]{1,0:T(8,128)(2,1)}, bf16[128,6144]{1,0:T(8,128)(2,1)}, bf16[2048,128]{1,0:T(8,128)(2,1)}, f32[128,1536]{1,0:T(8,128)}, f32[128...) custom-call(s32[1,8]{1,0:T(1,128)} %ids_ref.1, s32[1]{0:T(128)S(6)} %copy.19.len_ref, ...), custom_call_target="tpu_custom_call" | custom-call | tf_op jit(solution)/shard_map/policy_update/pallas_call | solution.py:529
  77.6 3.8 %hand_over.1 = (bf16[256,128]{1,0:T(8,128)(2,1)}, bf16[128,6144]{1,0:T(8,128)(2,1)}, bf16[2048,128]{1,0:T(8,128)(2,1)}, f32[128,1536]{1,0:T(8,128)}, f32[128,153...) custom-call(bf16[256,128]{1,0:T(8,128)(2,1)} %get-tuple-element.14.refs_0_, ...), custom_call_target="tpu_custom_call" | custom-call | tf_op jit(solution)/shard_map/hand_over/pallas_call | solution.py:582

commit v3 on v2

--- a/solution.py
+++ b/solution.py
@@ -56,9 +56,11 @@
     dec_out, nq_out, no_out, mq_out, sq_out, mo_out, so_out,
     table, keys, vals, wq, wout, m_q, v_q, m_o, v_o, cot,
     tsend, trecv, gsend, grecv, idx4, idsend, idrecv, selsend, selrecv,
-    xsend, xrecv, hrs, hrrecv, rsend, rmsg, agrecv, nq, no, dec,
+    xsend, xrecv, hrs, hrrecv, hsend, hmsg, hgrecv, rsend, rmsg, agrecv,
+    count_mix, count_grad, nq, no, dec,
     loc, out_sem, id_s, id_r, idg_s, idg_r, ts_s, ts_r, gs_s, gs_r,
-    cot_s, cot_r, sel_s, sel_r, x_s, x_r, rel_s, rel_r, ag_s, ag_r, hr_s, hr_r,
+    cot_s, cot_r, sel_s, sel_r, x_s, x_r, hrel_s, hrel_r, rel_s, rel_r,
+    hg_s, hg_r, ag_s, ag_r, hr_s, hr_r,
     e_s, e_r,
 ):
     role = lax.axis_index("role")
@@ -188,12 +190,6 @@
 
     @pl.when(holder)
     def _():
-        settle(trecv, ts_r)
-
-        def add(k, total):
-            return total + trecv[k].astype(F32)
-        total = lax.fori_loop(0, 31, add, tsend[my_unit].astype(F32))
-        whole = total.astype(BF16)
         settle(idrecv.at[0:31], idg_r)
         got = idrecv[...].astype(F32)
         got = jnp.concatenate([
@@ -201,6 +197,12 @@
             jnp.broadcast_to(got[:, :, 64:65], (32, 16, 128))], axis=1).reshape(1024, 128)
         lane = lax.broadcasted_iota(jnp.int32, (1024, 128), 1) + 128 * (my_unit % 2)
         chosen = jnp.where(got == lane.astype(F32), 1.0, 0.0).astype(BF16)
+        settle(trecv, ts_r)
+
+        def add(k, total):
+            return total + trecv[k].astype(F32)
+        total = lax.fori_loop(0, 31, add, tsend[my_unit].astype(F32))
+        whole = total.astype(BF16)
         selsend[...] = nn(chosen, whole).astype(BF16).reshape(32, 32, 128)
 
         def send_rows(k, p, h, u):
@@ -211,6 +213,8 @@
     @pl.when(role == LEARNER)
     def _():
         each_peer(lambda k, p, h, u: put(gsend.at[p], grecv.at[k - 1], gs_s, gs_r, role, p))
+        for q in range(3):
+            put(cot_hbm, cot, cot_s.at[q], cot_r, q, shard)
     send_ids(False)
 
     @pl.when(holder)
@@ -275,6 +279,14 @@
 
     @pl.when(role == LEARNER)
     def _():
+        live_out = [jnp.where(live8, t, 0.0) for t in out_tiles]
+        for q in range(4):
+            for i in range(2):
+                hsend[q, :, i * 128:(i + 1) * 128] = stack(
+                    [live_out[4 * q + i], live_out[4 * q + 2 + i]]).astype(BF16)
+        for q in range(3):
+            put(hsend.at[q], hmsg, hrel_s.at[q], hrel_r, q, shard)
+        hmsg[...] = hsend[3]
         settle(grecv, gs_r)
         g_tiles = [None] * 16
         for i in range(8):
@@ -299,93 +311,122 @@
         ]
         gp += [gk[8 * h:8 * h + 8] for h in range(16)]
         gp += [gv[8 * h:8 * h + 8] for h in range(16)]
-        live_out = [jnp.where(live8, t, 0.0) for t in out_tiles]
         for q in range(4):
             tiles = [(gp[12 * q + i], gp[12 * q + 6 + i]) for i in range(6)]
-            tiles += [(live_out[4 * q + i], live_out[4 * q + 2 + i]) for i in range(2)]
             for i, pair in enumerate(tiles):
                 rsend[q, :, i * 128:(i + 1) * 128] = stack(pair).astype(BF16)
         for q in range(3):
             put(rsend.at[q], rmsg, rel_s.at[q], rel_r, q, shard)
-        for q in range(3):
-            put(cot_hbm, cot, cot_s.at[q], cot_r, q, shard)
+
         rmsg[...] = rsend[3]
 
     def shard_at(py, px, pz):
         return (py % 4) * 8 + (px % 4) * 2 + pz % 2
 
     class Gather:
-        def __init__(self, msg, buf, send, recv):
-            self.msg, self.buf, self.send, self.recv = msg, buf, send, recv
+        def __init__(self, msg, buf, send, recv, count):
+            self.msg, self.buf, self.send, self.recv, self.count = msg, buf, send, recv, count
+
+        def lanes(self, half):
+            width = self.msg.shape[1] // 2
+            return pl.ds(half * width, width)
 
         def hop(self, step, half, src, dst, dy, dx, dz):
-            put(src, dst, self.send, self.recv.at[half, step], role,
+            put(src, dst, self.send.at[half], self.recv.at[half, step], role,
                 shard_at(y + dy, x + dx, zl + dz))
 
+        def arrived(self, half, step, blocks):
+            settle(self.count.at[0:blocks], self.recv.at[half, step])
+
+        def start(self, far):
+            self.buf[y, x, zl] = self.msg[...]
+            for half in range(2):
+                n = self.lanes(half)
+                spots = [(0, 1), (1, 0), (3, 0), (1, 1), (3, 1)] + far
+                for d, dz in spots:
+                    self.hop(0, half, self.msg.at[:, n], self.buf.at[y, x, zl, :, n],
+                             d * half, d * (1 - half), dz)
+
+        def line(self, half):
+            n = self.lanes(half)
+            return self.buf.at[:, x, :, :, n] if half else self.buf.at[y, :, :, :, n]
+
+        def sent(self):
+            for half in range(2):
+                settle(self.count.at[0:31], self.send.at[half])
+
+    class Short(Gather):
         def first(self):
-            self.buf[y, x, zl] = self.msg[...]
-            for half in range(2):
-                lanes = pl.ds(half * 512, 512)
-                for d, dz in ((1, 0), (3, 0), (0, 1), (1, 1), (3, 1)):
-                    self.hop(0, half, self.msg.at[:, lanes], self.buf.at[y, x, zl, :, lanes],
-                             d * half, d * (1 - half), dz)
+            self.start([(2, 0), (2, 1)])
 
         def second(self):
             for half in range(2):
-                settle(selrecv.at[0:10], self.recv.at[half, 0])
-                lanes = pl.ds(half * 512, 512)
+                self.arrived(half, 0, 7)
+                for d in (2, 1, 3):
+                    self.hop(1, half, self.line(half), self.line(half),
+                             d * (1 - half), d * half, 0)
+
+        def last(self):
+            for half in range(2):
+                self.arrived(half, 1, 24)
+
+    class Long(Gather):
+        def first(self):
+            self.start([])
+
+        def second(self):
+            for half in range(2):
+                self.arrived(half, 0, 5)
+                n = self.lanes(half)
                 dy, dx = half, 1 - half
-                before = self.buf.at[(y + 3 * dy) % 4, (x + 3 * dx) % 4, zl, :, lanes]
-                after = self.buf.at[(y + dy) % 4, (x + dx) % 4, 1 - zl, :, lanes]
+                before = self.buf.at[(y + 3 * dy) % 4, (x + 3 * dx) % 4, zl, :, n]
+                after = self.buf.at[(y + dy) % 4, (x + dx) % 4, 1 - zl, :, n]
                 self.hop(1, half, before, before, dy, dx, 0)
                 self.hop(1, half, after, after, 3 * dy, 3 * dx, 0)
 
         def third(self):
             for half in range(2):
-                settle(trecv.at[0:1], self.recv.at[half, 1])
-                lanes = pl.ds(half * 512, 512)
-                line = self.buf.at[:, x, :, :, lanes] if half else self.buf.at[y, :, :, :, lanes]
+                self.arrived(half, 1, 2)
                 for d in (1, 3):
-                    self.hop(2, half, line, line, d * (1 - half), d * half, 0)
+                    self.hop(2, half, self.line(half), self.line(half),
+                             d * (1 - half), d * half, 0)
 
         def fourth(self):
             for half in range(2):
-                settle(trecv.at[0:8], self.recv.at[half, 2])
-                lanes = pl.ds(half * 512, 512)
+                self.arrived(half, 2, 16)
+                n = self.lanes(half)
                 if half:
-                    before = self.buf.at[0:2, (x + 3) % 4, :, :, lanes]
-                    after = self.buf.at[2:4, (x + 1) % 4, :, :, lanes]
+                    before = self.buf.at[0:2, (x + 3) % 4, :, :, n]
+                    after = self.buf.at[2:4, (x + 1) % 4, :, :, n]
                 else:
-                    before = self.buf.at[(y + 3) % 4, 0:2, :, :, lanes]
-                    after = self.buf.at[(y + 1) % 4, 2:4, :, :, lanes]
+                    before = self.buf.at[(y + 3) % 4, 0:2, :, :, n]
+                    after = self.buf.at[(y + 1) % 4, 2:4, :, :, n]
                 self.hop(3, half, before, before, 1 - half, half, 0)
                 self.hop(3, half, after, after, 3 * (1 - half), 3 * half, 0)
 
         def last(self):
             for half in range(2):
-                settle(trecv.at[0:4], self.recv.at[half, 3])
-
-        def sent(self):
-            settle(trecv, self.send)
-
-    mixes = Gather(hrs, hrrecv, hr_s, hr_r)
-    grads = Gather(rmsg, agrecv, ag_s, ag_r)
+                self.arrived(half, 3, 8)
+
+    mixes = Long(hrs, hrrecv, hr_s, hr_r, count_mix)
+    heads = Short(hmsg, hgrecv, hg_s, hg_r, idrecv)
+    grads = Short(rmsg, agrecv, ag_s, ag_r, count_grad)
 
     @pl.when(role != LEARNER)
     def _():
+        settle(hmsg, hrel_r)
+        heads.first()
         mixes.first()
         settle(rmsg, rel_r)
     grads.first()
 
     @pl.when(role == LEARNER)
     def _():
+        heads.first()
         mixes.first()
+    heads.second()
     grads.second()
-    grads.third()
     mixes.second()
-    grads.fourth()
-    mixes.third()
-    grads.last()
 
     got_ids = idrecv[...].astype(F32)[:, 8:16, 64:65]
     got_ids = jnp.broadcast_to(
@@ -395,7 +436,7 @@
     low = jnp.where(got_ids == lane, 1.0, 0.0).astype(BF16)
     high = jnp.where(got_ids == lane + 128.0, 1.0, 0.0).astype(BF16)
     rows = nn(low, table[0:128, :]) + nn(high, table[128:256, :])
-    halves = [jnp.where(half == j, rows, 0.0).astype(BF16) for j in range(2)]
+    halves = [jnp.where(half == j, rows, 0.0).T.astype(BF16) for j in range(2)]
     for f in fetches[6:]:
         f.wait()
 
@@ -407,8 +448,8 @@
         copies.append(c)
 
     def spread(src, dst, n):
+        put(src, dst, e_s.at[1, n], e_r.at[1, n], across, shard)
         put(src, dst, e_s.at[0, n], e_r.at[0, n], sibling, shard)
-        put(src, dst, e_s.at[1, n], e_r.at[1, n], across, shard)
         copy_out(src, dst)
 
     def q_cols(of, c):
@@ -416,16 +457,6 @@
 
     def o_rows(of):
         return no_out.at[pl.ds(pl.multiple_of(of * 512, 128), 512), :]
-
-    for c in range(N_CHUNK):
-        j, at = divmod(c * CHUNK, 768)
-        cols = slice(c * CHUNK, (c + 1) * CHUNK)
-        grad = tn(halves[j], agrecv[:, :, :, :, at:at + CHUNK].reshape(512, CHUNK))
-        new, one, two = adamw(wq[:, cols], grad, m_q[:, cols], v_q[:, cols])
-        nq[:, cols] = new.astype(BF16)
-        m_q[:, cols] = one
-        v_q[:, cols] = two
-        spread(nq.at[:, cols], q_cols(role, c), c)
 
     @pl.when(role != LEARNER)
     def _():
@@ -434,7 +465,8 @@
         cot[...].astype(F32).reshape(32, 1, 8, 128), (32, 2, 8, 128)).reshape(512, 128)
     cot_both = jnp.concatenate(
         [jnp.where(half == j, cot_wide, 0.0).astype(BF16) for j in range(2)], axis=1)
-    grad_out = tn(agrecv[:, :, :, :, 768:1024].reshape(512, 256), cot_both)
+    heads.last()
+    grad_out = tn(hgrecv[...].reshape(512, 256), cot_both)
     for j in range(2):
         here = slice(j * 256, (j + 1) * 256)
         params = wout[pl.ds(pl.multiple_of(row0 + j * 256, 128), 256), :]
@@ -444,17 +476,28 @@
         m_o[here, :] = one
         v_o[here, :] = two
     spread(no, o_rows(role), N_CHUNK)
+    copy_out(m_o, mo_out)
+    copy_out(v_o, so_out)
+    mixes.third()
+
+    grads.last()
+    for c in range(N_CHUNK):
+        j, at = divmod(c * CHUNK, 768)
+        cols = slice(c * CHUNK, (c + 1) * CHUNK)
+        grad = nn(halves[j], agrecv[:, :, :, :, at:at + CHUNK].reshape(512, CHUNK))
+        new, one, two = adamw(wq[:, cols], grad, m_q[:, cols], v_q[:, cols])
+        nq[:, cols] = new.astype(BF16)
+        m_q[:, cols] = one
+        v_q[:, cols] = two
+        spread(nq.at[:, cols], q_cols(role, c), c)
     copy_out(m_q, mq_out)
     copy_out(v_q, sq_out)
-    copy_out(m_o, mo_out)
-    copy_out(v_o, so_out)
-
     mixes.fourth()
 
     def part(of, n):
         return q_cols(of, n) if n < N_CHUNK else o_rows(of)
 
-    for n in range(N_CHUNK + 1):
+    for n in (N_CHUNK, *range(N_CHUNK)):
         settle(part(across, n), e_r.at[1, n])
         put(part(across, n), part(across, n), e_s.at[2, n], e_r.at[2, n], sibling, shard)
 
@@ -490,8 +533,10 @@
         for q in range(3):
             settle(cot, cot_s.at[q])
             settle(rmsg, rel_s.at[q])
+            settle(hmsg, hrel_s.at[q])
         settle(gsend.at[0:31], gs_s)
     settle(idrecv.at[0:31], idg_s)
+    heads.sent()
     grads.sent()
     mixes.sent()
 
@@ -555,9 +600,14 @@
             vm((4, 16, 768), BF16),
             vm((16, 1024), BF16),
             vm((4, 4, 2, 16, 1024), BF16),
-            vm((4, 16, 1024), BF16),
-            vm((16, 1024), BF16),
-            vm((4, 4, 2, 16, 1024), BF16),
+            vm((4, 16, 256), BF16),
+            vm((16, 256), BF16),
+            vm((4, 4, 2, 16, 256), BF16),
+            vm((4, 16, 768), BF16),
+            vm((16, 768), BF16),
+            vm((4, 4, 2, 16, 768), BF16),
+            vm((31, 16, 512), BF16),
+            vm((31, 16, 384), BF16),
             vm((128, 1536), BF16),
             vm((512, 128), BF16),
             vm((256, 128), BF16),
@@ -571,8 +621,10 @@
             dma, dma,
             dma((3,)), dma((3,)),
             dma((3,)), dma,
-            dma, dma((2, 4)),
-            dma, dma((2, 4)),
+            dma((3,)), dma,
+            dma((2,)), dma((2, 2)),
+            dma((2,)), dma((2, 2)),
+            dma((2,)), dma((2, 4)),
             dma((3, N_CHUNK + 1)), dma((3, N_CHUNK + 1)),
         ],
         compiler_params=pltpu.CompilerParams(

time: 81.6 us -> 75.7 us (0.928)
  Pallas kernels: 80.2 us -> 73.7 us
    pallas_call x1, Pallas kernels: 76.4 us -> 69.8 us  [shards(): pl.pallas_call(kernel, out_shape=tuple((jax.ShapeDtypeStruct(*a) for a in...]
where the time goes in v3:
time: 75.7 us; the launch traced here: 74.9 us
  Pallas kernels  73.7 us (97%)
  between operations  1.29 us (2%)
    pallas_call x1, Pallas kernels, shards(): pl.pallas_call(kernel, out_shape=tuple((jax.ShapeDtypeStruct(*a) for a in...  69.8 us
    pallas_call x1, Pallas kernels, shards(): pl.pallas_call(hand_over, out_shape=tuple((jax.ShapeDtypeStruct(*a) for a...  3.84 us

profile of v3, /device:TPU:1, one launch (start us, length us, event | category | flops | bytes accessed | tf_op | source)
XLA Modules:
  0.0 74.9 jit_solution(9180436359223133247)
XLA Ops:
  1.3 69.8 %policy_update.1 = (bf16[256,128]{1,0:T(8,128)(2,1)}, bf16[128,6144]{1,0:T(8,128)(2,1)}, bf16[2048,128]{1,0:T(8,128)(2,1)}, f32[128,1536]{1,0:T(8,128)}, f32[128...) custom-call(s32[1,8]{1,0:T(1,128)} %ids_ref.1, s32[1]{0:T(128)S(6)} %copy.19.len_ref, ...), custom_call_target="tpu_custom_call" | custom-call | tf_op jit(solution)/shard_map/policy_update/pallas_call | solution.py:574
  71.1 3.8 %hand_over.1 = (bf16[256,128]{1,0:T(8,128)(2,1)}, bf16[128,6144]{1,0:T(8,128)(2,1)}, bf16[2048,128]{1,0:T(8,128)(2,1)}, f32[128,1536]{1,0:T(8,128)}, f32[128,153...) custom-call(bf16[256,128]{1,0:T(8,128)(2,1)} %get-tuple-element.14.refs_0_, ...), custom_call_target="tpu_custom_call" | custom-call | tf_op jit(solution)/shard_map/hand_over/pallas_call | solution.py:634

commit v4 on v3

--- a/solution.py
+++ b/solution.py
@@ -21,8 +21,8 @@
 scale = HD ** (-0.5)
 
 N_CHUNK = 4
+CHUNKS = ((0, 256), (768, 256), (256, 512), (1024, 512))
 ORDER = 13
-CHUNK = 1536 // N_CHUNK
 
 
 def adamw(params, gradient, first_moment, second_moment):
@@ -56,28 +56,40 @@
     dec_out, nq_out, no_out, mq_out, sq_out, mo_out, so_out,
     table, keys, vals, wq, wout, m_q, v_q, m_o, v_o, cot,
     tsend, trecv, gsend, grecv, idx4, idsend, idrecv, selsend, selrecv,
-    xsend, xrecv, hrs, hrrecv, hsend, hmsg, hgrecv, rsend, rmsg, agrecv,
+    xsend, xrecv, hrs, hrrecv, hsend, hmsg, hgrecv, rsend_a, rsend_b, rmsg_a, rmsg_b,
+    agrecv_a, agrecv_b,
     count_mix, count_grad, nq, no, dec,
     loc, out_sem, id_s, id_r, idg_s, idg_r, ts_s, ts_r, gs_s, gs_r,
-    cot_s, cot_r, sel_s, sel_r, x_s, x_r, hrel_s, hrel_r, rel_s, rel_r,
-    hg_s, hg_r, ag_s, ag_r, hr_s, hr_r,
+    cot_s, cot_r, sel_s, sel_r, x_s, x_r, hrel_s, hrel_r, rela_s, rela_r, relb_s, relb_r,
+    hg_s, hg_r, aga_s, aga_r, agb_s, agb_r, hr_s, hr_r,
     e_s, e_r,
 ):
     role = lax.axis_index("role")
     shard = lax.axis_index("shard")
-    y, x, zl = shard // 8, (shard // 2) % 4, shard % 2
-    z_hi, core = role // 2, role % 2
+    y, x, zl = shard >> 3, (shard >> 1) & 3, shard & 1
+    z_hi, core = role >> 1, role & 1
     sibling = z_hi * 2 + (1 - core)
     across = (1 - z_hi) * 2 + core
+    others = [(role + q) & 3 for q in range(4)]
+
+    ys = [(y + d) & 3 for d in range(4)]
+    xs = [(x + d) & 3 for d in range(4)]
+    zs = [zl, 1 - zl]
+    spots = [(x + y + d) & 3 for d in range(4)]
+    holds = [spot < 3 for spot in spots]
+    rows_at = [v * 8 for v in ys]
+    cols_at = [v * 2 for v in xs]
+    unit_row = [v * 6 for v in ys]
+    unit_col = [v * 2 for v in spots]
 
     def peer(k):
-        py, px, pz = (y + k // 8) % 4, (x + (k // 2) % 4) % 4, (zl + k % 2) % 2
-        spot = (px + py) % 4
-        return py * 8 + px * 2 + pz, spot < 3, py * 6 + spot * 2 + pz
-
-    my_spot = (x + y) % 4
-    holder = my_spot < 3
-    my_unit = jnp.where(holder, y * 6 + my_spot * 2 + zl, 0)
+        dy, dx, dz = k >> 3, (k >> 1) & 3, k & 1
+        turn = (dy + dx) & 3
+        return (rows_at[dy] + cols_at[dx] + zs[dz], holds[turn],
+                unit_row[dy] + unit_col[turn] + zs[dz])
+
+    holder = holds[0]
+    my_unit = jnp.where(holder, peer(0)[2], 0)
 
     def put(src, dst, send, recv, to_role, to_shard):
         pltpu.make_async_remote_copy(
@@ -86,18 +98,16 @@
         ).start()
 
     def each_peer(body, first=1, last=32):
-        def step(j, carry):
-            k = (j * ORDER) % 32
+        for j in range(first, last):
+            k = j * ORDER % 32
             body(k, *peer(k))
-            return carry
-        lax.fori_loop(first, last, step, 0)
 
     barrier = pltpu.get_barrier_semaphore()
     each_peer(lambda k, p, h, u: pl.semaphore_signal(
         barrier, inc=1, device_id=(role, p), device_id_type=MESH))
     for q in range(1, 4):
         pl.semaphore_signal(
-            barrier, inc=1, device_id=((role + q) % 4, shard), device_id_type=MESH)
+            barrier, inc=1, device_id=(others[q], shard), device_id_type=MESH)
 
     col0 = pl.multiple_of(role * 1536, 128)
     row0 = pl.multiple_of(role * 512, 128)
@@ -144,7 +154,7 @@
     pl.semaphore_wait(barrier, 34)
 
     for q in range(1, 4):
-        put(idx4.at[role], idx4.at[role], id_s.at[q - 1], id_r.at[q - 1], (role + q) % 4, shard)
+        put(idx4.at[role], idx4.at[role], id_s.at[q - 1], id_r.at[q - 1], others[q], shard)
 
     def send_part(k, p, h, u):
         @pl.when(h)
@@ -195,7 +205,7 @@
         got = jnp.concatenate([
             jnp.broadcast_to(got[:, :, 0:1], (32, 16, 128)),
             jnp.broadcast_to(got[:, :, 64:65], (32, 16, 128))], axis=1).reshape(1024, 128)
-        lane = lax.broadcasted_iota(jnp.int32, (1024, 128), 1) + 128 * (my_unit % 2)
+        lane = lax.broadcasted_iota(jnp.int32, (1024, 128), 1) + 128 * (my_unit & 1)
         chosen = jnp.where(got == lane.astype(F32), 1.0, 0.0).astype(BF16)
         settle(trecv, ts_r)
 
@@ -233,9 +243,10 @@
                 [blocks[i][8 * q:8 * q + 8], blocks[6 + i][8 * q:8 * q + 8]], axis=0)
             xsend[q, :, i * 128:(i + 1) * 128] = pair.astype(BF16)
     for q in range(1, 4):
-        to = (role + q) % 4
+        to = others[q]
         put(xsend.at[to], xrecv.at[role], x_s.at[q - 1], x_r.at[q - 1], to, shard)
     xrecv[role] = xsend[role]
+
     fetches[4].wait()
     fetches[5].wait()
     for q in range(1, 4):
@@ -287,6 +298,111 @@
         for q in range(3):
             put(hsend.at[q], hmsg, hrel_s.at[q], hrel_r, q, shard)
         hmsg[...] = hsend[3]
+
+    @pl.when(role != LEARNER)
+    def _():
+        settle(hmsg, hrel_r)
+    def shard_at(py, px, pz):
+        return rows_at[py] + cols_at[px] + zs[pz]
+
+    class Gather:
+        def __init__(self, msg, buf, send, recv, count):
+            self.msg, self.buf, self.send, self.recv, self.count = msg, buf, send, recv, count
+
+        def lanes(self, half):
+            width = self.msg.shape[1] // 2
+            return pl.ds(half * width, width)
+
+        def hop(self, step, half, src, dst, dy, dx, dz):
+            put(src, dst, self.send.at[half], self.recv.at[half, step], role,
+                shard_at(dy, dx, dz))
+
+        def arrived(self, half, step, blocks):
+            settle(self.count.at[0:blocks], self.recv.at[half, step])
+
+        def start(self, far):
+            self.buf[y, x, zl] = self.msg[...]
+            for half in range(2):
+                n = self.lanes(half)
+                spots = [(0, 1), (1, 0), (3, 0), (1, 1), (3, 1)] + far
+                for d, dz in spots:
+                    self.hop(0, half, self.msg.at[:, n], self.buf.at[y, x, zl, :, n],
+                             d * half, d * (1 - half), dz)
+
+        def line(self, half):
+            n = self.lanes(half)
+            return self.buf.at[:, x, :, :, n] if half else self.buf.at[y, :, :, :, n]
+
+        def sent(self):
+            for half in range(2):
+                settle(self.count.at[0:31], self.send.at[half])
+
+    class Short(Gather):
+        def first(self):
+            self.start([(2, 0), (2, 1)])
+
+        def second(self):
+            for half in range(2):
+                self.arrived(half, 0, 7)
+                for d in (2, 1, 3):
+                    self.hop(1, half, self.line(half), self.line(half),
+                             d * (1 - half), d * half, 0)
+
+        def last(self):
+            for half in range(2):
+                self.arrived(half, 1, 24)
+
+    class Long(Gather):
+        def first(self):
+            self.start([])
+
+        def second(self):
+            for half in range(2):
+                self.arrived(half, 0, 5)
+                n = self.lanes(half)
+                dy, dx = half, 1 - half
+                before = self.buf.at[ys[3 * dy], xs[3 * dx], zl, :, n]
+                after = self.buf.at[ys[dy], xs[dx], 1 - zl, :, n]
+                self.hop(1, half, before, before, dy, dx, 0)
+                self.hop(1, half, after, after, 3 * dy, 3 * dx, 0)
+
+        def third(self):
+            for half in range(2):
+                self.arrived(half, 1, 2)
+                for d in (1, 3):
+                    self.hop(2, half, self.line(half), self.line(half),
+                             d * (1 - half), d * half, 0)
+
+        def fourth(self):
+            for half in range(2):
+                self.arrived(half, 2, 16)
+                n = self.lanes(half)
+                if half:
+                    before = self.buf.at[0:2, xs[3], :, :, n]
+                    after = self.buf.at[2:4, xs[1], :, :, n]
+                else:
+                    before = self.buf.at[ys[3], 0:2, :, :, n]
+                    after = self.buf.at[ys[1], 2:4, :, :, n]
+                self.hop(3, half, before, before, 1 - half, half, 0)
+                self.hop(3, half, after, after, 3 * (1 - half), 3 * half, 0)
+
+        def last(self):
+            for half in range(2):
+                self.arrived(half, 3, 8)
+
+    mixes = Long(hrs, hrrecv, hr_s, hr_r, count_mix)
+    heads = Short(hmsg, hgrecv, hg_s, hg_r, idrecv)
+    grads_a = Short(rmsg_a, agrecv_a, aga_s, aga_r, idrecv)
+    grads_b = Short(rmsg_b, agrecv_b, agb_s, agb_r, count_grad)
+
+    heads.first()
+
+    @pl.when(role != LEARNER)
+    def _():
+        mixes.first()
+
+    @pl.when(role == LEARNER)
+    def _():
         settle(grecv, gs_r)
         g_tiles = [None] * 16
         for i in range(8):
@@ -312,184 +428,108 @@
         gp += [gk[8 * h:8 * h + 8] for h in range(16)]
         gp += [gv[8 * h:8 * h + 8] for h in range(16)]
         for q in range(4):
-            tiles = [(gp[12 * q + i], gp[12 * q + 6 + i]) for i in range(6)]
-            for i, pair in enumerate(tiles):
-                rsend[q, :, i * 128:(i + 1) * 128] = stack(pair).astype(BF16)
+            for i in range(6):
+                pair = stack([gp[12 * q + i], gp[12 * q + 6 + i]]).astype(BF16)
+                if i < 2:
+                    rsend_a[q, :, i * 128:(i + 1) * 128] = pair
+                else:
+                    rsend_b[q, :, (i - 2) * 128:(i - 1) * 128] = pair
         for q in range(3):
-            put(rsend.at[q], rmsg, rel_s.at[q], rel_r, q, shard)
-
-        rmsg[...] = rsend[3]
-
-    def shard_at(py, px, pz):
-        return (py % 4) * 8 + (px % 4) * 2 + pz % 2
-
-    class Gather:
-        def __init__(self, msg, buf, send, recv, count):
-            self.msg, self.buf, self.send, self.recv, self.count = msg, buf, send, recv, count
-
-        def lanes(self, half):
-            width = self.msg.shape[1] // 2
-            return pl.ds(half * width, width)
-
-        def hop(self, step, half, src, dst, dy, dx, dz):
-            put(src, dst, self.send.at[half], self.recv.at[half, step], role,
-                shard_at(y + dy, x + dx, zl + dz))
-
-        def arrived(self, half, step, blocks):
-            settle(self.count.at[0:blocks], self.recv.at[half, step])
-
-        def start(self, far):
-            self.buf[y, x, zl] = self.msg[...]
-            for half in range(2):
-                n = self.lanes(half)
-                spots = [(0, 1), (1, 0), (3, 0), (1, 1), (3, 1)] + far
-                for d, dz in spots:
-                    self.hop(0, half, self.msg.at[:, n], self.buf.at[y, x, zl, :, n],
-                             d * half, d * (1 - half), dz)
-
-        def line(self, half):
-            n = self.lanes(half)
-            return self.buf.at[:, x, :, :, n] if half else self.buf.at[y, :, :, :, n]
-
-        def sent(self):
-            for half in range(2):
-                settle(self.count.at[0:31], self.send.at[half])
-
-    class Short(Gather):
-        def first(self):
-            self.start([(2, 0), (2, 1)])
-
-        def second(self):
-            for half in range(2):
-                self.arrived(half, 0, 7)
-                for d in (2, 1, 3):
-                    self.hop(1, half, self.line(half), self.line(half),
-                             d * (1 - half), d * half, 0)
-
-        def last(self):
-            for half in range(2):
-                self.arrived(half, 1, 24)
-
-    class Long(Gather):
-        def first(self):
-            self.start([])
-
-        def second(self):
-            for half in range(2):
-                self.arrived(half, 0, 5)
-                n = self.lanes(half)
-                dy, dx = half, 1 - half
-                before = self.buf.at[(y + 3 * dy) % 4, (x + 3 * dx) % 4, zl, :, n]
-                after = self.buf.at[(y + dy) % 4, (x + dx) % 4, 1 - zl, :, n]
-                self.hop(1, half, before, before, dy, dx, 0)
-                self.hop(1, half, after, after, 3 * dy, 3 * dx, 0)
-
-        def third(self):
-            for half in range(2):
-                self.arrived(half, 1, 2)
-                for d in (1, 3):
-                    self.hop(2, half, self.line(half), self.line(half),
-                             d * (1 - half), d * half, 0)
-
-        def fourth(self):
-            for half in range(2):
-                self.arrived(half, 2, 16)
-                n = self.lanes(half)
-                if half:
-                    before = self.buf.at[0:2, (x + 3) % 4, :, :, n]
-                    after = self.buf.at[2:4, (x + 1) % 4, :, :, n]
-                else:
-                    before = self.buf.at[(y + 3) % 4, 0:2, :, :, n]
-                    after = self.buf.at[(y + 1) % 4, 2:4, :, :, n]
-                self.hop(3, half, before, before, 1 - half, half, 0)
-                self.hop(3, half, after, after, 3 * (1 - half), 3 * half, 0)
-
-        def last(self):
-            for half in range(2):
-                self.arrived(half, 3, 8)
-
-    mixes = Long(hrs, hrrecv, hr_s, hr_r, count_mix)
-    heads = Short(hmsg, hgrecv, hg_s, hg_r, idrecv)
-    grads = Short(rmsg, agrecv, ag_s, ag_r, count_grad)
+            put(rsend_a.at[q], rmsg_a, rela_s.at[q], rela_r, q, shard)
+        for q in range(3):
+            put(rsend_b.at[q], rmsg_b, relb_s.at[q], relb_r, q, shard)
+        rmsg_a[...] = rsend_a[3]
+        rmsg_b[...] = rsend_b[3]
+
+    copies = []
+
+    def copy_out(a, b):
+        pltpu.make_async_copy(a, b, out_sem.at[len(copies)]).start()
+        copies.append(a)
+
+    def spread(src, dst, n):
+        put(src, dst, e_s.at[1, n], e_r.at[1, n], across, shard)
+        put(src, dst, e_s.at[0, n], e_r.at[0, n], sibling, shard)
+        copy_out(src, dst)
+
+    def q_cols(of, n):
+        at, width = CHUNKS[n]
+        return nq_out.at[:, pl.ds(pl.multiple_of(of * 1536 + at, 128), width)]
+
+    def o_rows(of):
+        return no_out.at[pl.ds(pl.multiple_of(of * 512, 128), 512), :]
+
+    half = (lax.broadcasted_iota(jnp.int32, (512, 128), 0) // 8) % 2
+
+    def update_out():
+        copies.clear()
+        fetches[8].wait()
+        fetches[9].wait()
+        cot_wide = jnp.broadcast_to(
+            cot[...].astype(F32).reshape(32, 1, 8, 128), (32, 2, 8, 128)).reshape(512, 128)
+        cot_both = jnp.concatenate(
+            [jnp.where(half == j, cot_wide, 0.0).astype(BF16) for j in range(2)], axis=1)
+        heads.last()
+        grad_out = tn(hgrecv[...].reshape(512, 256), cot_both)
+        for j in range(2):
+            here = slice(j * 256, (j + 1) * 256)
+            params = wout[pl.ds(pl.multiple_of(row0 + j * 256, 128), 256), :]
+            new, one, two = adamw(
+                params, grad_out[:, j * 128:(j + 1) * 128], m_o[here, :], v_o[here, :])
+            no[here, :] = new.astype(BF16)
+            m_o[here, :] = one
+            v_o[here, :] = two
+        spread(no, o_rows(role), N_CHUNK)
+        copy_out(m_o, mo_out)
+        copy_out(v_o, so_out)
 
     @pl.when(role != LEARNER)
     def _():
-        settle(hmsg, hrel_r)
-        heads.first()
+        settle(rmsg_a, rela_r)
+    grads_a.first()
+
+    @pl.when(role != LEARNER)
+    def _():
+        settle(rmsg_b, relb_r)
+    grads_b.first()
+    heads.second()
+    grads_a.second()
+    grads_b.second()
+
+    @pl.when(role == LEARNER)
+    def _():
         mixes.first()
-        settle(rmsg, rel_r)
-    grads.first()
-
-    @pl.when(role == LEARNER)
-    def _():
-        heads.first()
-        mixes.first()
-    heads.second()
-    grads.second()
+
+    @pl.when(role != LEARNER)
+    def _():
+        settle(cot, cot_r)
     mixes.second()
+    update_out()
 
     got_ids = idrecv[...].astype(F32)[:, 8:16, 64:65]
     got_ids = jnp.broadcast_to(
         jnp.concatenate([got_ids, got_ids], axis=1), (32, 16, 128)).reshape(512, 128)
     lane = lax.broadcasted_iota(jnp.int32, (512, 128), 1).astype(F32)
-    half = (lax.broadcasted_iota(jnp.int32, (512, 128), 0) // 8) % 2
     low = jnp.where(got_ids == lane, 1.0, 0.0).astype(BF16)
     high = jnp.where(got_ids == lane + 128.0, 1.0, 0.0).astype(BF16)
     rows = nn(low, table[0:128, :]) + nn(high, table[128:256, :])
     halves = [jnp.where(half == j, rows, 0.0).T.astype(BF16) for j in range(2)]
-    for f in fetches[6:]:
-        f.wait()
-
-    copies = []
-
-    def copy_out(a, b):
-        c = pltpu.make_async_copy(a, b, out_sem.at[len(copies)])
-        c.start()
-        copies.append(c)
-
-    def spread(src, dst, n):
-        put(src, dst, e_s.at[1, n], e_r.at[1, n], across, shard)
-        put(src, dst, e_s.at[0, n], e_r.at[0, n], sibling, shard)
-        copy_out(src, dst)
-
-    def q_cols(of, c):
-        return nq_out.at[:, pl.ds(pl.multiple_of(of * 1536 + c * CHUNK, 128), CHUNK)]
-
-    def o_rows(of):
-        return no_out.at[pl.ds(pl.multiple_of(of * 512, 128), 512), :]
-
-    @pl.when(role != LEARNER)
-    def _():
-        settle(cot, cot_r)
-    cot_wide = jnp.broadcast_to(
-        cot[...].astype(F32).reshape(32, 1, 8, 128), (32, 2, 8, 128)).reshape(512, 128)
-    cot_both = jnp.concatenate(
-        [jnp.where(half == j, cot_wide, 0.0).astype(BF16) for j in range(2)], axis=1)
-    heads.last()
-    grad_out = tn(hgrecv[...].reshape(512, 256), cot_both)
-    for j in range(2):
-        here = slice(j * 256, (j + 1) * 256)
-        params = wout[pl.ds(pl.multiple_of(row0 + j * 256, 128), 256), :]
-        new, one, two = adamw(
-            params, grad_out[:, j * 128:(j + 1) * 128], m_o[here, :], v_o[here, :])
-        no[here, :] = new.astype(BF16)
-        m_o[here, :] = one
-        v_o[here, :] = two
-    spread(no, o_rows(role), N_CHUNK)
-    copy_out(m_o, mo_out)
-    copy_out(v_o, so_out)
-    mixes.third()
-
-    grads.last()
-    for c in range(N_CHUNK):
-        j, at = divmod(c * CHUNK, 768)
-        cols = slice(c * CHUNK, (c + 1) * CHUNK)
-        grad = nn(halves[j], agrecv[:, :, :, :, at:at + CHUNK].reshape(512, CHUNK))
+    fetches[6].wait()
+    fetches[7].wait()
+    for n, (at, width) in enumerate(CHUNKS):
+        cols = slice(at, at + width)
+        if n == 0:
+            grads_a.last()
+        if n == 2:
+            mixes.third()
+            grads_b.last()
+        buf = agrecv_b if n >= 2 else agrecv_a
+        grad = nn(halves[n % 2], buf[...].reshape(512, width))
         new, one, two = adamw(wq[:, cols], grad, m_q[:, cols], v_q[:, cols])
         nq[:, cols] = new.astype(BF16)
         m_q[:, cols] = one
         v_q[:, cols] = two
-        spread(nq.at[:, cols], q_cols(role, c), c)
+        spread(nq.at[:, cols], q_cols(role, n), n)
     copy_out(m_q, mq_out)
     copy_out(v_q, sq_out)
     mixes.fourth()
@@ -513,8 +553,8 @@
         settle(part((1 - z_hi) * 2 + (1 - core), n), e_r.at[2, n])
         for way in range(3):
             settle(part(role, n), e_s.at[way, n])
-    for c in copies:
-        c.wait()
+    for i, a in enumerate(copies):
+        settle(a, out_sem.at[i])
     for q in range(3):
         settle(idx4.at[0], id_s.at[q])
         settle(xsend.at[0], x_s.at[q])
@@ -532,12 +572,14 @@
     def _():
         for q in range(3):
             settle(cot, cot_s.at[q])
-            settle(rmsg, rel_s.at[q])
+            settle(rmsg_a, rela_s.at[q])
+            settle(rmsg_b, relb_s.at[q])
             settle(hmsg, hrel_s.at[q])
         settle(gsend.at[0:31], gs_s)
     settle(idrecv.at[0:31], idg_s)
     heads.sent()
-    grads.sent()
+    grads_a.sent()
+    grads_b.sent()
     mixes.sent()
 
 
@@ -603,11 +645,14 @@
             vm((4, 16, 256), BF16),
             vm((16, 256), BF16),
             vm((4, 4, 2, 16, 256), BF16),
-            vm((4, 16, 768), BF16),
-            vm((16, 768), BF16),
-            vm((4, 4, 2, 16, 768), BF16),
+            vm((4, 16, 256), BF16),
+            vm((4, 16, 512), BF16),
+            vm((16, 256), BF16),
+            vm((16, 512), BF16),
+            vm((4, 4, 2, 16, 256), BF16),
+            vm((4, 4, 2, 16, 512), BF16),
             vm((31, 16, 512), BF16),
-            vm((31, 16, 384), BF16),
+            vm((31, 16, 256), BF16),
             vm((128, 1536), BF16),
             vm((512, 128), BF16),
             vm((256, 128), BF16),
@@ -622,6 +667,8 @@
             dma((3,)), dma((3,)),
             dma((3,)), dma,
             dma((3,)), dma,
+            dma((3,)), dma,
+            dma((2,)), dma((2, 2)),
             dma((2,)), dma((2, 2)),
             dma((2,)), dma((2, 2)),
             dma((2,)), dma((2, 4)),

time: 75.7 us -> 73 us (0.964)
  Pallas kernels: 73.7 us -> 71.6 us
    pallas_call x1, Pallas kernels: 69.8 us -> 67.8 us  [shards(): pl.pallas_call(kernel, out_shape=tuple((jax.ShapeDtypeStruct(*a) for a in...]
where the time goes in v4:
time: 73 us; the launch traced here: 72.9 us
  Pallas kernels  71.6 us (98%)
  between operations  1.29 us (2%)
    pallas_call x1, Pallas kernels, shards(): pl.pallas_call(kernel, out_shape=tuple((jax.ShapeDtypeStruct(*a) for a in...  67.8 us
    pallas_call x1, Pallas kernels, shards(): pl.pallas_call(hand_over, out_shape=tuple((jax.ShapeDtypeStruct(*a) for a...  3.84 us

profile of v4, /device:TPU:1, one launch (start us, length us, event | category | flops | bytes accessed | tf_op | source)
XLA Modules:
  0.0 72.9 jit_solution(281538401030829718)
XLA Ops:
  1.3 67.8 %policy_update.1 = (bf16[256,128]{1,0:T(8,128)(2,1)}, bf16[128,6144]{1,0:T(8,128)(2,1)}, bf16[2048,128]{1,0:T(8,128)(2,1)}, f32[128,1536]{1,0:T(8,128)}, f32[128...) custom-call(s32[1,8]{1,0:T(1,128)} %ids_ref.1, s32[1]{0:T(128)S(6)} %copy.19.len_ref, ...), custom_call_target="tpu_custom_call" | custom-call | tf_op jit(solution)/shard_map/policy_update/pallas_call | solution.py:616
  69.0 3.8 %hand_over.1 = (bf16[256,128]{1,0:T(8,128)(2,1)}, bf16[128,6144]{1,0:T(8,128)(2,1)}, bf16[2048,128]{1,0:T(8,128)(2,1)}, f32[128,1536]{1,0:T(8,128)}, f32[128,153...) custom-call(bf16[256,128]{1,0:T(8,128)(2,1)} %get-tuple-element.14.refs_0_, ...), custom_call_target="tpu_custom_call" | custom-call | tf_op jit(solution)/shard_map/hand_over/pallas_call | solution.py:681

commit v5 on v4

--- a/solution.py
+++ b/solution.py
@@ -22,6 +22,7 @@
 
 N_CHUNK = 4
 CHUNKS = ((0, 256), (768, 256), (256, 512), (1024, 512))
+MIDDLE = BF16
 ORDER = 13
 
 
@@ -55,11 +56,11 @@
     m_q_hbm, v_q_hbm, m_o_hbm, v_o_hbm, cot_hbm,
     dec_out, nq_out, no_out, mq_out, sq_out, mo_out, so_out,
     table, keys, vals, wq, wout, m_q, v_q, m_o, v_o, cot,
-    tsend, trecv, gsend, grecv, idx4, idsend, idrecv, selsend, selrecv,
+    tsend, line_in, line_sum, line_out, plane_in, gsend, grecv, idx4, idsend, idrecv, selsend, selrecv,
     xsend, xrecv, hrs, hrrecv, hsend, hmsg, hgrecv, rsend_a, rsend_b, rmsg_a, rmsg_b,
     agrecv_a, agrecv_b,
     count_mix, count_grad, nq, no, dec,
-    loc, out_sem, id_s, id_r, idg_s, idg_r, ts_s, ts_r, gs_s, gs_r,
+    loc, out_sem, id_s, id_r, idg_s, idg_r, ts_s, ts_r, tp_s, tp_r, gs_s, gs_r,
     cot_s, cot_r, sel_s, sel_r, x_s, x_r, hrel_s, hrel_r, rela_s, rela_r, relb_s, relb_r,
     hg_s, hg_r, aga_s, aga_r, agb_s, agb_r, hr_s, hr_r,
     e_s, e_r,
@@ -148,19 +149,22 @@
     fetches[1].wait()
     for c in range(12):
         part = nn(table[...], wq[:, c * 128:(c + 1) * 128]).astype(BF16)
-        tsend[2 * c] = part[0:128]
-        tsend[2 * c + 1] = part[128:256]
+        for h in range(2):
+            u = 2 * c + h
+            row, spot, pz = u // 6, u % 6 // 2, u % 2
+            tsend[0, u] = part[h * 128:h * 128 + 64]
+            tsend[1, (spot - row) % 4 * 6 + spot * 2 + pz] = part[h * 128 + 64:h * 128 + 128]
 
     pl.semaphore_wait(barrier, 34)
 
     for q in range(1, 4):
         put(idx4.at[role], idx4.at[role], id_s.at[q - 1], id_r.at[q - 1], others[q], shard)
 
-    def send_part(k, p, h, u):
-        @pl.when(h)
-        def _():
-            put(tsend.at[u], trecv.at[k - 1], ts_s, ts_r, role, p)
-    each_peer(send_part, 1, 12)
+    for d in (2, 1, 3):
+        put(tsend.at[0, pl.ds(ys[d] * 6, 6)], line_in.at[0, d - 1], ts_s.at[0], ts_r.at[0],
+            role, rows_at[d] + cols_at[0] + zs[0])
+        put(tsend.at[1, pl.ds(xs[d] * 6, 6)], line_in.at[1, d - 1], ts_s.at[1], ts_r.at[1],
+            role, rows_at[0] + cols_at[d] + zs[0])
 
     for q in range(1, 4):
         settle(idx4.at[0], id_r.at[q - 1])
@@ -179,7 +183,20 @@
                 put(idsend, idrecv.at[shard], idg_s, idg_r, role, p)
         each_peer(body)
     send_ids(True)
-    each_peer(send_part, 12, 32)
+
+    for half in range(2):
+        settle(line_in.at[half], ts_r.at[half])
+        total = tsend[half, pl.ds((xs[0] if half else ys[0]) * 6, 6)].astype(F32)
+        for d in range(3):
+            total += line_in[half, d].astype(F32)
+        line_sum[half] = total
+        line_out[half] = total.astype(line_out.dtype)
+        for d, dz in ((2, 0), (2, 1), (1, 1), (3, 1), (1, 0), (3, 0), (0, 1)):
+            @pl.when(holds[d])
+            def _():
+                put(line_out.at[half, spots[d] * 2 + zs[dz]], plane_in.at[half, d * 2 + dz - 1],
+                    tp_s.at[half], tp_r.at[half], role,
+                    (rows_at[d] + cols_at[0] if half else rows_at[0] + cols_at[d]) + zs[dz])
 
     @pl.when(role == LEARNER)
     def _():
@@ -207,12 +224,14 @@
             jnp.broadcast_to(got[:, :, 64:65], (32, 16, 128))], axis=1).reshape(1024, 128)
         lane = lax.broadcasted_iota(jnp.int32, (1024, 128), 1) + 128 * (my_unit & 1)
         chosen = jnp.where(got == lane.astype(F32), 1.0, 0.0).astype(BF16)
-        settle(trecv, ts_r)
-
-        def add(k, total):
-            return total + trecv[k].astype(F32)
-        total = lax.fori_loop(0, 31, add, tsend[my_unit].astype(F32))
-        whole = total.astype(BF16)
+        parts = []
+        for half in range(2):
+            settle(plane_in.at[half], tp_r.at[half])
+            total = line_sum[half, spots[0] * 2 + zl]
+            for k in range(7):
+                total += plane_in[half, k].astype(F32)
+            parts.append(total)
+        whole = jnp.concatenate(parts, axis=0).astype(BF16)
         selsend[...] = nn(chosen, whole).astype(BF16).reshape(32, 32, 128)
 
         def send_rows(k, p, h, u):
@@ -561,12 +580,14 @@
 
     @pl.when(holder)
     def _():
-        settle(tsend.at[0:23], ts_s)
+        for half in range(2):
+            settle(plane_in.at[half, 0:5], tp_s.at[half])
         settle(selsend.at[0:31], sel_s)
 
     @pl.when(jnp.logical_not(holder))
     def _():
-        settle(tsend, ts_s)
+        for half in range(2):
+            settle(plane_in.at[half, 0:6], tp_s.at[half])
 
     @pl.when(role == LEARNER)
     def _():
@@ -577,6 +598,8 @@
             settle(hmsg, hrel_s.at[q])
         settle(gsend.at[0:31], gs_s)
     settle(idrecv.at[0:31], idg_s)
+    for half in range(2):
+        settle(line_in.at[half], ts_s.at[half])
     heads.sent()
     grads_a.sent()
     grads_b.sent()
@@ -629,8 +652,11 @@
             vm((512, 128), F32),
             vm((512, 128), F32),
             vm((256, 128), BF16),
-            vm((24, 128, 128), BF16),
-            vm((31, 128, 128), BF16),
+            vm((2, 24, 64, 128), BF16),
+            vm((2, 3, 6, 64, 128), BF16),
+            vm((2, 6, 64, 128), F32),
+            vm((2, 6, 64, 128), MIDDLE),
+            vm((2, 7, 64, 128), MIDDLE),
             vm((32, 16, 1024), BF16),
             vm((31, 16, 1024), BF16),
             vm((4, 8, 128), F32),
@@ -660,7 +686,8 @@
             dma((N_CHUNK + 6,)),
             dma((3,)), dma((3,)),
             dma, dma,
-            dma, dma,
+            dma((2,)), dma((2,)),
+            dma((2,)), dma((2,)),
             dma, dma,
             dma((3,)), dma,
             dma, dma,

time: 73 us -> 66.9 us (0.916)
  Pallas kernels: 71.6 us -> 65.4 us
    pallas_call x1, Pallas kernels: 67.8 us -> 61.6 us  [shards(): pl.pallas_call(kernel, out_shape=tuple((jax.ShapeDtypeStruct(*a) for a in...]
where the time goes in v5:
time: 66.9 us; the launch traced here: 66.7 us
  Pallas kernels  65.4 us (98%)
  between operations  1.29 us (2%)
    pallas_call x1, Pallas kernels, shards(): pl.pallas_call(kernel, out_shape=tuple((jax.ShapeDtypeStruct(*a) for a in...  61.6 us
    pallas_call x1, Pallas kernels, shards(): pl.pallas_call(hand_over, out_shape=tuple((jax.ShapeDtypeStruct(*a) for a...  3.84 us

profile of v5, /device:TPU:1, one launch (start us, length us, event | category | flops | bytes accessed | tf_op | source)
XLA Modules:
  0.0 66.7 jit_solution(11685613618674350818)
XLA Ops:
  1.3 61.6 %policy_update.1 = (bf16[256,128]{1,0:T(8,128)(2,1)}, bf16[128,6144]{1,0:T(8,128)(2,1)}, bf16[2048,128]{1,0:T(8,128)(2,1)}, f32[128,1536]{1,0:T(8,128)}, f32[128...) custom-call(s32[1,8]{1,0:T(1,128)} %ids_ref.1, s32[1]{0:T(128)S(6)} %copy.19.len_ref, ...), custom_call_target="tpu_custom_call" | custom-call | tf_op jit(solution)/shard_map/policy_update/pallas_call | solution.py:639
  62.9 3.8 %hand_over.1 = (bf16[256,128]{1,0:T(8,128)(2,1)}, bf16[128,6144]{1,0:T(8,128)(2,1)}, bf16[2048,128]{1,0:T(8,128)(2,1)}, f32[128,1536]{1,0:T(8,128)}, f32[128,153...) custom-call(bf16[256,128]{1,0:T(8,128)(2,1)} %get-tuple-element.14.refs_0_, ...), custom_call_target="tpu_custom_call" | custom-call | tf_op jit(solution)/shard_map/hand_over/pallas_call | solution.py:708

commit v6 on v5

--- a/solution.py
+++ b/solution.py
@@ -56,11 +56,12 @@
     m_q_hbm, v_q_hbm, m_o_hbm, v_o_hbm, cot_hbm,
     dec_out, nq_out, no_out, mq_out, sq_out, mo_out, so_out,
     table, keys, vals, wq, wout, m_q, v_q, m_o, v_o, cot,
-    tsend, line_in, line_sum, line_out, plane_in, gsend, grecv, idx4, idsend, idrecv, selsend, selrecv,
+    tsend, line_in, line_sum, line_out, plane_in,
+    gsend, g_line, g_sum, g_out, g_plane, idx4, idsend, idrecv, selsend, selrecv,
     xsend, xrecv, hrs, hrrecv, hsend, hmsg, hgrecv, rsend_a, rsend_b, rmsg_a, rmsg_b,
     agrecv_a, agrecv_b,
     count_mix, count_grad, nq, no, dec,
-    loc, out_sem, id_s, id_r, idg_s, idg_r, ts_s, ts_r, tp_s, tp_r, gs_s, gs_r,
+    loc, out_sem, id_s, id_r, idg_s, idg_r, ts_s, ts_r, tp_s, tp_r, gs_s, gs_r, gp_s, gp_r,
     cot_s, cot_r, sel_s, sel_r, x_s, x_r, hrel_s, hrel_r, rela_s, rela_r, relb_s, relb_r,
     hg_s, hg_r, aga_s, aga_r, agb_s, agb_r, hr_s, hr_r,
     e_s, e_r,
@@ -208,8 +209,8 @@
                 .reshape(32, 8, 128)
                 for j in range(2)
             )
-            gsend[:, :, i * 128:(i + 1) * 128] = jnp.concatenate(
-                [upper, lower], axis=1).astype(BF16)
+            gsend[i // 4, :, :, :, :, i % 4 * 128:(i % 4 + 1) * 128] = jnp.concatenate(
+                [upper, lower], axis=1).astype(BF16).reshape(4, 4, 2, 16, 128)
 
     @pl.when(role != LEARNER)
     def _():
@@ -241,7 +242,11 @@
 
     @pl.when(role == LEARNER)
     def _():
-        each_peer(lambda k, p, h, u: put(gsend.at[p], grecv.at[k - 1], gs_s, gs_r, role, p))
+        for d in (2, 1, 3):
+            put(gsend.at[0, ys[d]], g_line.at[0, d - 1], gs_s.at[0], gs_r.at[0],
+                role, rows_at[d] + cols_at[0] + zs[0])
+            put(gsend.at[1, :, xs[d]], g_line.at[1, d - 1], gs_s.at[1], gs_r.at[1],
+                role, rows_at[0] + cols_at[d] + zs[0])
         for q in range(3):
             put(cot_hbm, cot, cot_s.at[q], cot_r, q, shard)
     send_ids(False)
@@ -265,6 +270,20 @@
         to = others[q]
         put(xsend.at[to], xrecv.at[role], x_s.at[q - 1], x_r.at[q - 1], to, shard)
     xrecv[role] = xsend[role]
+
+    @pl.when(role == LEARNER)
+    def _():
+        for half in range(2):
+            settle(g_line.at[half], gs_r.at[half])
+            total = (gsend[1, :, x] if half else gsend[0, y]).astype(F32)
+            for d in range(3):
+                total += g_line[half, d].astype(F32)
+            g_sum[half] = total
+            g_out[half] = total.astype(BF16)
+            for d, dz in ((2, 0), (2, 1), (1, 1), (3, 1), (1, 0), (3, 0), (0, 1)):
+                put(g_out.at[half, ys[d] if half else xs[d], zs[dz]],
+                    g_plane.at[half, d * 2 + dz - 1], gp_s.at[half], gp_r.at[half], role,
+                    (rows_at[d] + cols_at[0] if half else rows_at[0] + cols_at[d]) + zs[dz])
 
     fetches[4].wait()
     fetches[5].wait()
@@ -422,15 +441,16 @@
 
     @pl.when(role == LEARNER)
     def _():
-        settle(grecv, gs_r)
         g_tiles = [None] * 16
-        for i in range(8):
-            cols = slice(i * 128, (i + 1) * 128)
-            total = gsend[shard, :, cols].astype(F32)
-            for k in range(31):
-                total += grecv[k, :, cols].astype(F32)
-            g_tiles[i] = jnp.where(live8, total[0:8], 0.0)
-            g_tiles[8 + i] = jnp.where(live8, total[8:16], 0.0)
+        for half in range(2):
+            settle(g_plane.at[half], gp_r.at[half])
+            total = g_sum[half, y if half else x, zl]
+            for k in range(7):
+                total += g_plane[half, k].astype(F32)
+            for i in range(4):
+                cols = slice(i * 128, (i + 1) * 128)
+                g_tiles[4 * half + i] = jnp.where(live8, total[0:8, cols], 0.0)
+                g_tiles[8 + 4 * half + i] = jnp.where(live8, total[8:16, cols], 0.0)
         g_all = stack(g_tiles).astype(BF16)
         gw1 = stack([nt(g_tiles[h].astype(BF16), head(vals, h)) for h in range(16)])
         gw2 = nt(g_all, v_new)
@@ -596,7 +616,9 @@
             settle(rmsg_a, rela_s.at[q])
             settle(rmsg_b, relb_s.at[q])
             settle(hmsg, hrel_s.at[q])
-        settle(gsend.at[0:31], gs_s)
+        for half in range(2):
+            settle(g_line.at[half], gs_s.at[half])
+            settle(g_plane.at[half], gp_s.at[half])
     settle(idrecv.at[0:31], idg_s)
     for half in range(2):
         settle(line_in.at[half], ts_s.at[half])
@@ -657,8 +679,11 @@
             vm((2, 6, 64, 128), F32),
             vm((2, 6, 64, 128), MIDDLE),
             vm((2, 7, 64, 128), MIDDLE),
-            vm((32, 16, 1024), BF16),
-            vm((31, 16, 1024), BF16),
+            vm((2, 4, 4, 2, 16, 512), BF16),
+            vm((2, 3, 4, 2, 16, 512), BF16),
+            vm((2, 4, 2, 16, 512), F32),
+            vm((2, 4, 2, 16, 512), BF16),
+            vm((2, 7, 16, 512), BF16),
             vm((4, 8, 128), F32),
             vm((16, 128), BF16),
             vm((32, 16, 128), BF16),
@@ -688,7 +713,8 @@
             dma, dma,
             dma((2,)), dma((2,)),
             dma((2,)), dma((2,)),
-            dma, dma,
+            dma((2,)), dma((2,)),
+            dma((2,)), dma((2,)),
             dma((3,)), dma,
             dma, dma,
             dma((3,)), dma((3,)),

time: 66.9 us -> 64.8 us (0.969)
  Pallas kernels: 65.4 us -> 63.2 us
    pallas_call x1, Pallas kernels: 61.6 us -> 59.4 us  [shards(): pl.pallas_call(kernel, out_shape=tuple((jax.ShapeDtypeStruct(*a) for a in...]
where the time goes in v6:
time: 64.8 us; the launch traced here: 64.5 us
  Pallas kernels  63.2 us (98%)
  between operations  1.29 us (2%)
    pallas_call x1, Pallas kernels, shards(): pl.pallas_call(kernel, out_shape=tuple((jax.ShapeDtypeStruct(*a) for a in...  59.4 us
    pallas_call x1, Pallas kernels, shards(): pl.pallas_call(hand_over, out_shape=tuple((jax.ShapeDtypeStruct(*a) for a...  3.84 us

profile of v6, /device:TPU:1, one launch (start us, length us, event | category | flops | bytes accessed | tf_op | source)
XLA Modules:
  0.0 64.5 jit_solution(17125242119509377128)
XLA Ops:
  1.3 59.4 %policy_update.1 = (bf16[256,128]{1,0:T(8,128)(2,1)}, bf16[128,6144]{1,0:T(8,128)(2,1)}, bf16[2048,128]{1,0:T(8,128)(2,1)}, f32[128,1536]{1,0:T(8,128)}, f32[128...) custom-call(s32[1,8]{1,0:T(1,128)} %ids_ref.1, s32[1]{0:T(128)S(6)} %copy.19.len_ref, ...), custom_call_target="tpu_custom_call" | custom-call | tf_op jit(solution)/shard_map/policy_update/pallas_call | solution.py:661
  60.7 3.8 %hand_over.1 = (bf16[256,128]{1,0:T(8,128)(2,1)}, bf16[128,6144]{1,0:T(8,128)(2,1)}, bf16[2048,128]{1,0:T(8,128)(2,1)}, f32[128,1536]{1,0:T(8,128)}, f32[128,153...) custom-call(bf16[256,128]{1,0:T(8,128)(2,1)} %get-tuple-element.14.refs_0_, ...), custom_call_target="tpu_custom_call" | custom-call | tf_op jit(solution)/shard_map/hand_over/pallas_call | solution.py:734

commit v7 on v6

--- a/solution.py
+++ b/solution.py
@@ -61,7 +61,7 @@
     xsend, xrecv, hrs, hrrecv, hsend, hmsg, hgrecv, rsend_a, rsend_b, rmsg_a, rmsg_b,
     agrecv_a, agrecv_b,
     count_mix, count_grad, nq, no, dec,
-    loc, out_sem, id_s, id_r, idg_s, idg_r, ts_s, ts_r, tp_s, tp_r, gs_s, gs_r, gp_s, gp_r,
+    ready, loc, out_sem, id_s, id_r, idg_s, idg_r, ts_s, ts_r, tp_s, tp_r, gs_s, gs_r, gp_s, gp_r,
     cot_s, cot_r, sel_s, sel_r, x_s, x_r, hrel_s, hrel_r, rela_s, rela_r, relb_s, relb_r,
     hg_s, hg_r, aga_s, aga_r, agb_s, agb_r, hr_s, hr_r,
     e_s, e_r,
@@ -105,8 +105,8 @@
             body(k, *peer(k))
 
     barrier = pltpu.get_barrier_semaphore()
-    each_peer(lambda k, p, h, u: pl.semaphore_signal(
-        barrier, inc=1, device_id=(role, p), device_id_type=MESH))
+    for k in (1, 2, 3, 4, 5, 6, 7, 8, 16, 24):
+        pl.semaphore_signal(barrier, inc=1, device_id=(role, peer(k)[0]), device_id_type=MESH)
     for q in range(1, 4):
         pl.semaphore_signal(
             barrier, inc=1, device_id=(others[q], shard), device_id_type=MESH)
@@ -156,7 +156,9 @@
             tsend[0, u] = part[h * 128:h * 128 + 64]
             tsend[1, (spot - row) % 4 * 6 + spot * 2 + pz] = part[h * 128 + 64:h * 128 + 128]
 
-    pl.semaphore_wait(barrier, 34)
+    pl.semaphore_wait(barrier, 13)
+    for k in (8, 16, 24):
+        pl.semaphore_signal(ready, inc=1, device_id=(role, peer(k)[0]), device_id_type=MESH)
 
     for q in range(1, 4):
         put(idx4.at[role], idx4.at[role], id_s.at[q - 1], id_r.at[q - 1], others[q], shard)
@@ -183,6 +185,7 @@
             def _():
                 put(idsend, idrecv.at[shard], idg_s, idg_r, role, p)
         each_peer(body)
+    pl.semaphore_wait(ready, 3)
     send_ids(True)
 
     for half in range(2):
@@ -638,7 +641,7 @@
     ins, outs, stage, sems = refs[:7], refs[7:14], refs[14:21], refs[21]
     moves = []
     for a, v, b in zip(ins, stage, outs):
-        pieces = 4 if a.shape == (128, 6144) else 2 if a.shape[0] * a.shape[1] > 131072 else 1
+        pieces = 2 if a.shape == (128, 6144) else 1
         rows = a.shape[0] // pieces
         for i in range(pieces):
             part, n = pl.ds(i * rows, rows), len(moves)
@@ -707,6 +710,7 @@
             vm((128, 1536), BF16),
             vm((512, 128), BF16),
             vm((256, 128), BF16),
+            pltpu.SemaphoreType.REGULAR,
             dma((10,)),
             dma((N_CHUNK + 6,)),
             dma((3,)), dma((3,)),

time: 64.8 us -> 64.3 us (level)
  no operation moved by 1% of the time
where the time goes in v7:
time: 64.3 us; the launch traced here: 64.1 us
  Pallas kernels  62.9 us (98%)
  between operations  1.29 us (2%)
    pallas_call x1, Pallas kernels, shards(): pl.pallas_call(kernel, out_shape=tuple((jax.ShapeDtypeStruct(*a) for a in...  59.4 us
    pallas_call x1, Pallas kernels, shards(): pl.pallas_call(hand_over, out_shape=tuple((jax.ShapeDtypeStruct(*a) for a...  3.49 us

profile of v7, /device:TPU:1, one launch (start us, length us, event | category | flops | bytes accessed | tf_op | source)
XLA Modules:
  0.0 64.1 jit_solution(295926886885462328)
XLA Ops:
  1.3 59.4 %policy_update.1 = (bf16[256,128]{1,0:T(8,128)(2,1)}, bf16[128,6144]{1,0:T(8,128)(2,1)}, bf16[2048,128]{1,0:T(8,128)(2,1)}, f32[128,1536]{1,0:T(8,128)}, f32[128...) custom-call(s32[1,8]{1,0:T(1,128)} %ids_ref.1, s32[1]{0:T(128)S(6)} %copy.19.len_ref, ...), custom_call_target="tpu_custom_call" | custom-call | tf_op jit(solution)/shard_map/policy_update/pallas_call | solution.py:664
  60.7 3.5 %hand_over.1 = (bf16[256,128]{1,0:T(8,128)(2,1)}, bf16[128,6144]{1,0:T(8,128)(2,1)}, bf16[2048,128]{1,0:T(8,128)(2,1)}, f32[128,1536]{1,0:T(8,128)}, f32[128,153...) custom-call(bf16[256,128]{1,0:T(8,128)(2,1)} %get-tuple-element.14.refs_0_, ...), custom_call_target="tpu_custom_call" | custom-call | tf_op jit(solution)/shard_map/hand_over/pallas_call | solution.py:738

commit v8 on v7

--- a/solution.py
+++ b/solution.py
@@ -483,7 +483,7 @@
         rmsg_a[...] = rsend_a[3]
         rmsg_b[...] = rsend_b[3]
 
-    copies = []
+    copies, near = [], []
 
     def copy_out(a, b):
         pltpu.make_async_copy(a, b, out_sem.at[len(copies)]).start()
@@ -491,8 +491,8 @@
 
     def spread(src, dst, n):
         put(src, dst, e_s.at[1, n], e_r.at[1, n], across, shard)
-        put(src, dst, e_s.at[0, n], e_r.at[0, n], sibling, shard)
         copy_out(src, dst)
+        near.append((src, n))
 
     def q_cols(of, n):
         at, width = CHUNKS[n]
@@ -505,6 +505,7 @@
 
     def update_out():
         copies.clear()
+        near.clear()
         fetches[8].wait()
         fetches[9].wait()
         cot_wide = jnp.broadcast_to(
@@ -578,6 +579,9 @@
 
     def part(of, n):
         return q_cols(of, n) if n < N_CHUNK else o_rows(of)
+
+    for src, n in near:
+        put(src, part(role, n), e_s.at[0, n], e_r.at[0, n], sibling, shard)
 
     for n in (N_CHUNK, *range(N_CHUNK)):
         settle(part(across, n), e_r.at[1, n])

time: 64.3 us -> 64.3 us (level)
  no operation moved by 1% of the time
where the time goes in v8:
time: 64.3 us; the launch traced here: 64.1 us
  Pallas kernels  62.9 us (98%)
  between operations  1.29 us (2%)
    pallas_call x1, Pallas kernels, shards(): pl.pallas_call(kernel, out_shape=tuple((jax.ShapeDtypeStruct(*a) for a in...  59.4 us
    pallas_call x1, Pallas kernels, shards(): pl.pallas_call(hand_over, out_shape=tuple((jax.ShapeDtypeStruct(*a) for a...  3.49 us

profile of v8, /device:TPU:1, one launch (start us, length us, event | category | flops | bytes accessed | tf_op | source)
XLA Modules:
  0.0 64.1 jit_solution(2105899620122348689)
XLA Ops:
  1.3 59.4 %policy_update.1 = (bf16[256,128]{1,0:T(8,128)(2,1)}, bf16[128,6144]{1,0:T(8,128)(2,1)}, bf16[2048,128]{1,0:T(8,128)(2,1)}, f32[128,1536]{1,0:T(8,128)}, f32[128...) custom-call(s32[1,8]{1,0:T(1,128)} %ids_ref.1, s32[1]{0:T(128)S(6)} %copy.19.len_ref, ...), custom_call_target="tpu_custom_call" | custom-call | tf_op jit(solution)/shard_map/policy_update/pallas_call | solution.py:668
  60.7 3.5 %hand_over.1 = (bf16[256,128]{1,0:T(8,128)(2,1)}, bf16[128,6144]{1,0:T(8,128)(2,1)}, bf16[2048,128]{1,0:T(8,128)(2,1)}, f32[128,1536]{1,0:T(8,128)}, f32[128,153...) custom-call(bf16[256,128]{1,0:T(8,128)(2,1)} %get-tuple-element.14.refs_0_, ...), custom_call_target="tpu_custom_call" | custom-call | tf_op jit(solution)/shard_map/hand_over/pallas_call | solution.py:742
